TPU v7x, 32 devices: a whole 2x2x4 slice. The times are simulated.
32 devices in a mesh: view: 1, slab: 32 (over z, y, x, core).
Axes of the slice: x: 2, y: 2, z: 4, core: 2. Of those that a mesh axis runs over, the one named last changes fastest.
Arguments:
- image: float32 [128, 512, 512], P('slab'), may hold values from 0.1 to 10
- sensitivity: float32 [128, 512, 512], P('slab', 'view'), may hold values from 0.5 to 4
- resample_x: bfloat16 [2, 512, 512], P('view'), may hold values from 0 to 1, as said below
- resample_y: bfloat16 [2, 512, 512], P('view'), may hold values from 0 to 1, as said below
- tof_kernel: bfloat16 [2, 16, 512], P('view'), may hold values from 0.00019454956 to 0.0078125
- axial_mix: float32 [2, 128, 128], P('view'), may hold values from 0 to 1
- background: float32 [2, 16, 512, 128], P('view', None, 'slab'), may hold values from 0.5 to 2
- counts: int32 [2, 16, 512, 128], P('view', None, 'slab'), may hold values from 0 to 19
Outputs:
- new_image: float32 [128, 512, 512], P('slab', 'view')
Inputs may be any that keep to these rules, and one draw needn't show every extreme that they name: resample_x[v, a, x] is zero where |x - a| > 3. resample_y[v, y, b] is zero where |b - y| > 3.
All inputs are finite; a program needn't handle non-finite values.
Results may differ from a plain program's by a relative error of at most 0.00052.
Values may be sent and summed in bfloat16 or wider, within the bound.
No kernel may reach another device: no remote copies, remote signals or barrier semaphores. Data moves between devices by JAX's collectives and lax.ppermute only.
A program may use at most 64 MiB of HBM per device.

v0:
```python
import jax
import jax.numpy as jnp
from jax import lax
from jax.sharding import PartitionSpec as P


def local(image, sensitivity, resample_x, resample_y, tof_kernel, axial_mix, background, counts):
    highest = lax.Precision.HIGHEST
    image_low = image.astype(jnp.bfloat16)
    along_y = jnp.einsum(
        "zxy,vyb->vzxb", image_low, resample_y, preferred_element_type=jnp.float32
    ).astype(jnp.bfloat16)
    rotated = jnp.einsum(
        "vzxb,vax->vzba", along_y, resample_x, preferred_element_type=jnp.float32
    ).astype(jnp.bfloat16)
    gathered = lax.all_to_all(rotated, "slab", split_axis=2, concat_axis=1, tiled=True)
    integrals = jnp.einsum(
        "vka,vzba->vkbz", tof_kernel, gathered, preferred_element_type=jnp.float32
    )
    expected = background + jnp.einsum("vkbz,vcz->vkbc", integrals, axial_mix, precision=highest)
    ratios = counts.astype(jnp.float32) / expected
    back_mixed = jnp.einsum("vkbc,vcz->vkbz", ratios, axial_mix, precision=highest).astype(
        jnp.bfloat16
    )
    spread = jnp.einsum(
        "vka,vkbz->vzba", tof_kernel, back_mixed, preferred_element_type=jnp.float32
    ).astype(jnp.bfloat16)
    frames = lax.all_to_all(spread, "slab", split_axis=1, concat_axis=2, tiled=True)
    unrotated = jnp.einsum(
        "vzba,vyb->vzya", frames, resample_y, preferred_element_type=jnp.float32
    ).astype(jnp.bfloat16)
    own_rows = image.shape[1] // lax.axis_size("view")
    gradient = lax.psum_scatter(
        jnp.einsum("vzya,vax->xzy", unrotated, resample_x, preferred_element_type=jnp.float32),
        "view",
        scatter_dimension=0,
        tiled=True,
    )
    gradient = jnp.transpose(gradient, (1, 0, 2))
    current = lax.dynamic_slice_in_dim(image, lax.axis_index("view") * own_rows, own_rows, 1)
    return current * gradient / sensitivity


def solution(mesh):
    in_specs = (
        P("slab", None, None),
        P("slab", "view", None),
        P("view", None, None),
        P("view", None, None),
        P("view", None, None),
        P("view", None, None),
        P("view", None, "slab", None),
        P("view", None, "slab", None),
    )
    out_specs = P("slab", "view", None)
    return jax.shard_map(local, mesh=mesh, in_specs=in_specs, out_specs=out_specs, check_vma=False)
```

profile of v0, /device:TPU:0, one launch (start us, length us, event | category | flops | bytes accessed | tf_op | source)
XLA Modules:
  0.0 245.1 jit_solution(13615674045334650824)
XLA Ops:
  0.0 0.0 copy-start
  0.0 1.2 copy-done
  1.2 8.0 %fusion.9 = bf16[2,4,512,512]{3,2,1,0:T(8,128)(2,1)} fusion(f32[4,512,512]{2,1,0:T(8,128)} %param.8, bf16[2,512,512]{2,1,0:T(8,128)(2,1)S(1)} %copy-done, bf16[2,512,512]{2,1,0:T(8,128)(2,1)} %param.10), kind=kOutput, calls=%fused_computation.11 | convolution fusion | flops 4300210176 | bytes 10485760 | tf_op jit(solution)/shard_map/vzxb,vax->vzba/dot_general | solution.py:13
  9.2 5.4 %copy.28 = bf16[2,4,512,512]{3,1,0,2:T(4,128)(2,1)S(1)} copy(bf16[2,4,512,512]{3,2,1,0:T(8,128)(2,1)} %fusion.9) | data formatting | bytes 8388608 | tf_op jit(solution)/shard_map/convert_element_type | solution.py:15
  14.6 100.8 %all_to_all.36 = bf16[2,4,512,512]{3,1,0,2:T(4,128)(2,1)S(1)} all-to-all(bf16[2,4,512,512]{3,1,0,2:T(4,128)(2,1)S(1)} %copy.28), channel_id=1, replica_groups=mesh['view'=1,'slab'=32] {'slab'}, dimensions={2} | all-to-all | bytes 8388608 | tf_op jit(solution)/shard_map/all_to_all | solution.py:16
  115.4 1.4 copy.29
  116.8 0.0 copy-start.2
  116.8 0.6 copy.30
  117.5 0.1 copy-done.2
  117.6 1.2 convolution_bitcast_fusion
  118.8 0.8 copy.31
  119.6 0.0 copy-done.1
  119.6 1.4 fusion.24
  121.1 0.4 convolution_convert_fusion
  121.5 2.0 convert_bitcast_fusion
  123.6 4.4 %copy.33 = bf16[2,128,16,512]{3,2,0,1:T(8,128)(2,1)} copy(bf16[2,128,16,512]{3,1,2,0:T(8,128)(2,1)S(1)} %convert_bitcast_fusion) | data formatting | bytes 8388608 | tf_op jit(solution)/shard_map/convert_element_type | solution.py:27
  127.9 3.8 %all-to-all-start.1 = ((bf16[2,128,16,512]{3,2,0,1:T(8,128)(2,1)}), bf16[2,128,16,512]{3,2,0,1:T(8,128)(2,1)}, u32[]{:S(2)}, u32[]{:S(2)}) async-start(bf16[2,128,16,512]{3,2,0,1:T(8,128)(2,1)} %copy.33), calls=%async_computation.1 | async-start | bytes 8388608 | tf_op jit(solution)/shard_map/all_to_all | solution.py:28
  131.8 5.3 %copy.38 = f32[4,512,512]{1,2,0:T(8,128)} copy(f32[4,512,512]{2,1,0:T(8,128)} %param.8) | data formatting | bytes 8388608 | tf_op args[0]
  137.0 5.2 %copy.39 = f32[4,512,512]{1,2,0:T(8,128)} copy(f32[4,512,512]{2,1,0:T(8,128)} %param.9) | data formatting | bytes 8388608 | tf_op args[1]
  142.3 83.4 %all-to-all-done.1 = bf16[2,128,16,512]{3,2,0,1:T(8,128)(2,1)} async-done(((bf16[2,128,16,512]{3,2,0,1:T(8,128)(2,1)}), bf16[2,128,16,512]{3,2,0,1:T(8,128)(2,1)}, u32[]{:S(2)}, u32[]{:S(2)}) %all-to-all-start.1) | async-done | bytes 4194336 | tf_op jit(solution)/shard_map/all_to_all | solution.py:28
  225.6 4.9 %copy.35 = bf16[2,4,32,16,512]{4,3,2,1,0:T(8,128)(2,1)} copy(bf16[2,4,32,16,512]{4,3,0,1,2:T(8,128)(2,1)} %bitcast.16) | data formatting | bytes 8388608 | tf_op jit(solution)/shard_map/all_to_all | solution.py:28
  230.5 0.0 copy-done.3
  230.5 9.4 %fusion = f32[4,512,512]{1,2,0:T(8,128)} fusion(f32[4,512,512]{1,2,0:T(8,128)} %copy.39, f32[4,512,512]{1,2,0:T(8,128)} %copy.38, bf16[2,4,512,512]{3,2,1,0:T(8,128)(2,1)} %bitcast.69, bf16[2,512,512]{2,1,0:T(8,128)(2,1)S(1)} %copy-done.3, bf16[2,512,512]{2,1,0:T(8,128)(2,1)S(1)} %copy-done), kind=kOutput, calls=%fused_computation.1 | convolution fusion | flops 4299161600 | bytes 18874368 | tf_op jit(solution)/shard_map/vzya,vax->xzy/dot_general | solution.py:34
  239.9 5.2 %copy.40 = f32[4,512,512]{2,1,0:T(8,128)} copy(f32[4,512,512]{1,2,0:T(8,128)} %fusion) | data formatting | bytes 8388608 | tf_op jit(solution)/shard_map/div | solution.py:41
  (2 shorter events, 0.0 us)
Async XLA Ops:
  0.0 1.2 copy-start
  116.8 0.8 copy-start.2
  117.6 2.1 copy-start.1
  127.9 97.7 %all-to-all-start.1 = ((bf16[2,128,16,512]{3,2,0,1:T(8,128)(2,1)}), bf16[2,128,16,512]{3,2,0,1:T(8,128)(2,1)}, u32[]{:S(2)}, u32[]{:S(2)}) async-start(bf16[2,128,16,512]{3,2,0,1:T(8,128)(2,1)} %copy.33), calls=%async_computation.1 | async-start | bytes 8388608 | tf_op jit(solution)/shard_map/all_to_all | solution.py:28
  225.6 4.9 %copy-start.3 = (bf16[2,512,512]{2,1,0:T(8,128)(2,1)S(1)}, bf16[2,512,512]{2,1,0:T(8,128)(2,1)}, u32[]{:S(2)}) copy-start(bf16[2,512,512]{2,1,0:T(8,128)(2,1)} %param.10) | copy-start | bytes 3145732
where the time goes:
time: 246 us; the launch traced here: 245 us
  blocking collectives  101 us (41%)
  waiting for transfers between devices  83.4 us (34%)
  local copies, waits for them, and re-layouts  34.6 us (14%)
  matrix products  22.5 us (9%)
  starting transfers between devices  3.84 us (2%)
    all_to_all x1, blocking collectives, local(): lax.all_to_all(rotated, 'slab', split_axis=2, concat_axis=1, tiled=True)  101 us
    all_to_all x1, waiting for transfers between devices, local(): lax.all_to_all(spread, 'slab', split_axis=1, concat_axis=2, tiled=True)  83.4 us
    unnamed x10, local copies, waits for them, and re-layouts  11.8 us
    dot_general x1, matrix products, local(): jnp.einsum('vzya,vax->xzy', unrotated, resample_x, preferred_element_type...  9.37 us
    dot_general x1, matrix products, local(): jnp.einsum('vzxb,vax->vzba', along_y, resample_x, preferred_element_type=...  7.97 us
    convert_element_type x1, local copies, waits for them, and re-layouts, local(): rotated = jnp.einsum('vzxb,vax->vzba', along_y, resample_x, preferred_ele...  5.42 us
    div x1, local copies, waits for them, and re-layouts, local(): return current * gradient / sensitivity  5.22 us
  transfers between devices with their start and end apart: 1, of which 1 were waited for; matrix products, arithmetic and copies ran while one was open for 4% of the time, Pallas kernels for 0%

commit v1 on v0

v1 whole, which is shorter than its diff:
```python
import functools

import jax
import jax.numpy as jnp
from jax import lax
from jax.experimental import pallas as pl
from jax.experimental.pallas import tpu as pltpu
from jax.sharding import PartitionSpec as P

F32, BF16 = jnp.float32, jnp.bfloat16
VMEM_LIMIT = 56 * 1024 * 1024
NN = (((1,), (0,)), ((), ()))
NT = (((1,), (1,)), ((), ()))


def dot(a, b, dims=NN):
    return lax.dot_general(a, b, dims, preferred_element_type=F32)


def halves(x):
    high = x.astype(BF16)
    return high, (x - high.astype(F32)).astype(BF16)


def dot3(a, b, dims=NN):
    ah, al = halves(a)
    bh, bl = halves(b)
    return dot(ah, bh, dims) + (dot(ah, bl, dims) + dot(al, bh, dims))


def forward_kernel(views, slices, bins, image, rx, ry, tof, out, weights, partial):
    z = pl.program_id(0)
    rows = views * bins

    @pl.when(z == 0)
    def _():
        for v in range(views):
            high, low = halves(dot(tof[v], rx[v]))
            weights[v * bins : (v + 1) * bins] = high
            weights[rows + v * bins : rows + (v + 1) * bins] = low

    both = dot(weights[...], image[0].astype(BF16))
    partial[z] = both[:rows] + both[rows:]

    @pl.when(z == slices - 1)
    def _():
        per_view = []
        for v in range(views):
            mine = jnp.concatenate(
                [partial[s, v * bins : (v + 1) * bins] for s in range(slices)], axis=0
            )
            high, low = halves(mine)
            per_view.append(dot(high, ry[v]) + dot(low, ry[v]))
        joined = jnp.concatenate(
            [
                per_view[v][s * bins : (s + 1) * bins]
                for s in range(slices)
                for v in range(views)
            ],
            axis=0,
        )
        out[...] = joined.T


def swap_blocks(parts, width):
    n = len(parts)
    lane = lax.broadcasted_iota(jnp.int32, parts[0].shape, 1) // width
    step = 1
    while step < n:
        low = (lane // step) % 2 == 0
        new = list(parts)
        for i in range(n):
            if (i // step) % 2 == 0:
                a, b = parts[i], parts[i + step]
                shift = step * width
                new[i] = jnp.where(low, a, pltpu.roll(b, shift, 1))
                new[i + step] = jnp.where(
                    low, pltpu.roll(a, a.shape[1] - shift, 1), b
                )
        parts = new
        step *= 2
    return parts


def middle_kernel(views, slices, bins, owners, held, wire, mix, background, counts, out, turned, spread):
    rows = views * bins
    lanes = slices * rows
    blocks = []
    for first in range(0, held, slices):
        parts = [
            wire[pl.ds(first + i, owners, stride=held), :] for i in range(slices)
        ]
        blocks.append(jnp.concatenate(swap_blocks(parts, rows), axis=0).T)
    for v in range(views):
        turned[...] = mix[v].T
        mixed = jnp.concatenate(
            [turned[pl.ds(s, owners, stride=slices), :] for s in range(slices)], axis=0
        )
        sums = jnp.concatenate(
            [
                blocks[j // slices][
                    (j % slices) * rows + v * bins : (j % slices) * rows + (v + 1) * bins
                ]
                for j in range(held)
            ],
            axis=0,
        )
        base = v * bins * held
        added = jnp.concatenate(
            [background[pl.ds(base + j, bins, stride=held), :] for j in range(held)], axis=0
        )
        seen = jnp.concatenate(
            [counts[pl.ds(base + j, bins, stride=held), :] for j in range(held)], axis=0
        )
        ratios = seen.astype(F32) / (added + dot3(sums, mixed))
        back = dot3(mixed, ratios, NT)
        groups = held * bins // lanes
        for s in range(slices):
            for g in range(groups):
                spread[pl.ds((s * views + v) * groups + g, owners, stride=slices * views * groups), :] = back[
                    s * owners : (s + 1) * owners, g * lanes : (g + 1) * lanes
                ]
    out[...] = spread[...].astype(BF16)


def backward_kernel(views, slices, bins, owners, held, finish, *refs):
    if finish:
        wire, rxt, ry, tof, image, sensitivity, out, wide = refs
    else:
        wire, rxt, ry, tof, out, wide = refs
    z = pl.program_id(0)
    lanes = wire.shape[1]
    per_row = lanes // bins
    groups = held // per_row

    @pl.when(z == 0)
    def _():
        wide[...] = wire[...].astype(F32)

    mask = (
        lax.broadcasted_iota(jnp.int32, (per_row, lanes), 1) // bins
        == lax.broadcasted_iota(jnp.int32, (per_row, lanes), 0)
    )
    per_owner = slices * views * groups
    total = None
    for v in range(views):
        pieces = []
        for owner in range(owners):
            for g in range(groups):
                row = owner * per_owner + (z * views + v) * groups + g
                line = jnp.broadcast_to(wide[pl.ds(row, 1), :], (per_row, lanes))
                pieces.append(jnp.where(mask, line, 0.0))
        back = jnp.concatenate(pieces, axis=0).astype(BF16)
        frames = dot(back, tof[v]).astype(BF16)
        unrotated = dot(ry[v], frames).astype(BF16)
        term = dot(rxt[v], unrotated, NT)
        total = term if total is None else total + term
    if finish:
        out[0] = image[0] * total / sensitivity[0]
    else:
        out[0] = total


def local(view_size, image, sensitivity, resample_x, resample_y, tof_kernel, axial_mix, background, counts):
    views, bins, cells = tof_kernel.shape
    slices, nx, ny = image.shape
    held, planes = background.shape[2:]
    owners = planes // slices
    lanes = slices * views * bins
    params = pltpu.CompilerParams(
        dimension_semantics=("arbitrary",), vmem_limit_bytes=VMEM_LIMIT
    )
    whole = lambda x: pl.BlockSpec(x.shape, lambda z: (0,) * x.ndim)
    plane = pl.BlockSpec((1, nx, ny), lambda z: (z, 0, 0))

    rxt = jnp.swapaxes(resample_x, 1, 2)
    wire = pl.pallas_call(
        functools.partial(forward_kernel, views, slices, bins),
        grid=(slices,),
        in_specs=[plane, whole(resample_x), whole(resample_y), whole(tof_kernel)],
        out_specs=pl.BlockSpec((ny, lanes), lambda z: (0, 0)),
        out_shape=jax.ShapeDtypeStruct((ny, lanes), F32),
        scratch_shapes=[
            pltpu.VMEM((2 * views * bins, nx), BF16),
            pltpu.VMEM((slices, views * bins, ny), F32),
        ],
        compiler_params=params,
        name="project",
    )(image, resample_x, resample_y, tof_kernel)
    wire = lax.all_to_all(
        wire.reshape(owners, held, lanes), "slab", 0, 0, tiled=True
    ).reshape(ny, lanes)

    per_owner = slices * views * (held * bins // lanes)
    back = pl.pallas_call(
        functools.partial(middle_kernel, views, slices, bins, owners, held),
        out_shape=jax.ShapeDtypeStruct((owners * per_owner, lanes), BF16),
        scratch_shapes=[
            pltpu.VMEM((planes, planes), F32),
            pltpu.VMEM((owners * per_owner, lanes), F32),
        ],
        compiler_params=pltpu.CompilerParams(vmem_limit_bytes=VMEM_LIMIT),
        name="compare",
    )(
        wire,
        axial_mix,
        background.reshape(-1, planes),
        counts.reshape(-1, planes),
    )
    back = lax.all_to_all(
        back.reshape(owners, per_owner, lanes), "slab", 0, 0, tiled=True
    ).reshape(owners * per_owner, lanes)

    tiled_tof = jnp.tile(tof_kernel, (1, lanes // bins, 1))
    finish = view_size == 1
    operands = [back, rxt, resample_y, tiled_tof]
    specs = [whole(x) for x in operands]
    if finish:
        operands += [image, sensitivity]
        specs += [plane, plane]
    result = pl.pallas_call(
        functools.partial(backward_kernel, views, slices, bins, owners, held, finish),
        grid=(slices,),
        in_specs=specs,
        out_specs=plane,
        out_shape=jax.ShapeDtypeStruct((slices, nx, ny), F32),
        scratch_shapes=[pltpu.VMEM((owners * per_owner, lanes), F32)],
        compiler_params=params,
        name="backproject",
    )(*operands)
    if finish:
        return result
    gradient = lax.psum_scatter(result, "view", scatter_dimension=1, tiled=True)
    own_rows = nx // view_size
    current = lax.dynamic_slice_in_dim(image, lax.axis_index("view") * own_rows, own_rows, 1)
    return current * gradient / sensitivity


def solution(mesh):
    in_specs = (
        P("slab", None, None),
        P("slab", "view", None),
        P("view", None, None),
        P("view", None, None),
        P("view", None, None),
        P("view", None, None),
        P("view", None, "slab", None),
        P("view", None, "slab", None),
    )
    out_specs = P("slab", "view", None)
    return jax.shard_map(
        functools.partial(local, mesh.shape["view"]),
        mesh=mesh,
        in_specs=in_specs,
        out_specs=out_specs,
        check_vma=False,
    )
```

time: 246 us -> 48.8 us (0.20)
  blocking collectives: 101 us -> 18 us
  waiting for transfers between devices: 83.4 us -> 6.89 us
  local copies, waits for them, and re-layouts: 34.6 us -> 2.1 us
  matrix products: 22.5 us -> 0 us
  Pallas kernels: 0 us -> 18.8 us
    all_to_all x1, blocking collectives: 101 us -> 18 us  [local(): lax.all_to_all(wire.reshape(owners, held, lanes), 'slab', 0, 0, tiled=True)]
    all_to_all x1, waiting for transfers between devices: 83.4 us -> 6.89 us  [local(): lax.all_to_all(back.reshape(owners, per_owner, lanes), 'slab', 0, 0, tile...]
    dot_general x6 -> x0, matrix products: 22.5 us -> none  [the longest x1 9.37 us: local(): jnp.einsum('vzya,vax->xzy', unrotated, resample_x, preferred_element_type...]
    pallas_call x0 -> x3, Pallas kernels: none -> 18.8 us  [the longest x1 10.5 us: local(): pl.pallas_call(functools.partial(backward_kernel, views, slices, bins, ow...]
    unnamed x10 -> x7, local copies, waits for them, and re-layouts: 11.8 us -> 1.34 us
    convert_element_type x2 -> x0, local copies, waits for them, and re-layouts: 9.77 us -> none  [the longest x1 5.42 us: local(): rotated = jnp.einsum('vzxb,vax->vzba', along_y, resample_x, preferred_ele...]
    all_to_all x3 -> x0, local copies, waits for them, and re-layouts: 6.91 us -> none  [the longest x1 4.86 us: local(): lax.all_to_all(spread, 'slab', split_axis=1, concat_axis=2, tiled=True)]
    div x1 -> x0, local copies, waits for them, and re-layouts: 5.22 us -> none  [local(): return current * gradient / sensitivity]
  transfers between devices with their start and end apart: 1 -> 1, of which waited for: 1 -> 1; matrix products, arithmetic and copies ran while one was open for 4% -> 3% of each run, Pallas kernels for 0% -> 0%
where the time goes in v1:
time: 48.8 us; the launch traced here: 48.4 us
  Pallas kernels  18.8 us (39%)
  blocking collectives  18 us (37%)
  waiting for transfers between devices  6.89 us (14%)
  starting transfers between devices  2.58 us (5%)
  local copies, waits for them, and re-layouts  2.1 us (4%)
    all_to_all x1, blocking collectives, local(): lax.all_to_all(wire.reshape(owners, held, lanes), 'slab', 0, 0, tiled=True)  18 us
    pallas_call x1, Pallas kernels, local(): pl.pallas_call(functools.partial(backward_kernel, views, slices, bins, ow...  10.5 us
    all_to_all x1, waiting for transfers between devices, local(): lax.all_to_all(back.reshape(owners, per_owner, lanes), 'slab', 0, 0, tile...  6.89 us
    pallas_call x1, Pallas kernels, local(): pl.pallas_call(functools.partial(forward_kernel, views, slices, bins), gr...  5.51 us
    pallas_call x1, Pallas kernels, local(): pl.pallas_call(functools.partial(middle_kernel, views, slices, bins, owne...  2.75 us
    all_to_all x1, starting transfers between devices, local(): lax.all_to_all(back.reshape(owners, per_owner, lanes), 'slab', 0, 0, tile...  2.58 us
    unnamed x7, local copies, waits for them, and re-layouts  1.34 us
  transfers between devices with their start and end apart: 1, of which 1 were waited for; matrix products, arithmetic and copies ran while one was open for 3% of the time, Pallas kernels for 0%

profile of v1, /device:TPU:0, one launch (start us, length us, event | category | flops | bytes accessed | tf_op | source)
XLA Modules:
  0.0 48.4 jit_solution(11977767357897922557)
XLA Ops:
  0.0 0.0 copy-start.2
  0.0 0.0 copy-start
  0.0 5.5 %project.1 = f32[512,128]{1,0:T(8,128)} custom-call(f32[4,512,512]{2,1,0:T(8,128)} %refs_4_.1, bf16[2,512,512]{2,1,0:T(8,128)(2,1)} %rx.1, bf16[2,512,512]{2,1,0:T(8,128)(2,1)} %refs_2_.1, bf16[2,16,512]{2,1,0:T(8,128)(2,1)} %tof.1), custom_call_target="tpu_custom_call" | custom-call | tf_op jit(solution)/shard_map/project/pallas_call | solution.py:177
  5.5 18.0 %all_to_all.10 = f32[32,16,128]{2,1,0:T(8,128)} all-to-all(f32[32,16,128]{2,1,0:T(8,128)} %bitcast.10), channel_id=1, replica_groups=mesh['view'=1,'slab'=32] {'slab'}, dimensions={0} | all-to-all | bytes 524288 | tf_op jit(solution)/shard_map/all_to_all | solution.py:190
  23.5 2.7 %compare.1 = bf16[512,128]{1,0:T(8,128)(2,1)} custom-call(f32[512,128]{1,0:T(8,128)} %bitcast.11, f32[2,128,128]{2,1,0:T(8,128)} %mix.1, f32[512,128]{1,0:T(8,128)} %bitcast.14, s32[512,128]{1,0:T(8,128)} %bitcast.15), custom_call_target="tpu_custom_call" | custom-call | tf_op jit(solution)/shard_map/compare/pallas_call | solution.py:195
  26.3 2.6 %all-to-all-start.1 = ((bf16[32,16,128]{2,1,0:T(8,128)(2,1)}), bf16[32,16,128]{2,1,0:T(8,128)(2,1)S(1)}, u32[]{:S(2)}, u32[]{:S(2)}) async-start(bf16[32,16,128]{2,1,0:T(8,128)(2,1)} %bitcast.13), calls=%async_computation.1 | async-start | bytes 262144 | tf_op jit(solution)/shard_map/all_to_all | solution.py:210
  28.9 0.0 copy-done
  28.9 1.3 %copy.9 = bf16[2,512,512]{1,2,0:T(8,128)(2,1)} copy(bf16[2,512,512]{2,1,0:T(8,128)(2,1)S(1)} %copy-done) | data formatting | bytes 2097152 | tf_op args[2]
  30.2 6.9 %all-to-all-done.1 = bf16[32,16,128]{2,1,0:T(8,128)(2,1)S(1)} async-done(((bf16[32,16,128]{2,1,0:T(8,128)(2,1)}), bf16[32,16,128]{2,1,0:T(8,128)(2,1)S(1)}, u32[]{:S(2)}, u32[]{:S(2)}) %all-to-all-start.1) | async-done | bytes 131104 | tf_op jit(solution)/shard_map/all_to_all | solution.py:210
  37.1 0.0 copy-start.1
  37.1 0.0 copy-done.2
  37.1 0.8 %tile.4 = bf16[2,8,16,512]{3,2,1,0:T(8,128)(2,1)} broadcast(bf16[2,16,512]{2,1,0:T(8,128)(2,1)S(1)} %copy-done.2), dimensions={0,2,3} | broadcast | bytes 294912 | tf_op jit(solution)/shard_map/tile | solution.py:214
  37.9 0.0 copy-done.1
  37.9 10.5 %backproject.1 = f32[4,512,512]{2,1,0:T(8,128)} custom-call(bf16[512,128]{1,0:T(8,128)(2,1)} %bitcast.12, bf16[2,512,512]{2,1,0:T(8,128)(2,1)} %bitcast.8, bf16[2,512,512]{2,1,0:T(8,128)(2,1)} %refs_2_.1, bf16[2,128,512]{2,1,0:T(8,128)(2,1)} %bitcast.9, f32[4,512,512]{2,1,0:T(8,128)} %refs_4_.1, f32[4,512,512]{2,1,0:T(8,128)} %refs_5_.1), custom_call_target="tpu_custom_call" | custom-call | tf_op jit(solution)/shard_map/backproject/pallas_call | solution.py:221
Async XLA Ops:
  0.0 37.1 %copy-start.2 = (bf16[2,16,512]{2,1,0:T(8,128)(2,1)S(1)}, bf16[2,16,512]{2,1,0:T(8,128)(2,1)}, u32[]{:S(2)}) copy-start(bf16[2,16,512]{2,1,0:T(8,128)(2,1)} %tof.1) | copy-start | bytes 98308
  0.0 28.9 %copy-start = (bf16[2,512,512]{2,1,0:T(8,128)(2,1)S(1)}, bf16[2,512,512]{2,1,0:T(8,128)(2,1)}, u32[]{:S(2)}) copy-start(bf16[2,512,512]{2,1,0:T(8,128)(2,1)} %rx.1) | copy-start | bytes 3145732
  26.3 10.8 %all-to-all-start.1 = ((bf16[32,16,128]{2,1,0:T(8,128)(2,1)}), bf16[32,16,128]{2,1,0:T(8,128)(2,1)S(1)}, u32[]{:S(2)}, u32[]{:S(2)}) async-start(bf16[32,16,128]{2,1,0:T(8,128)(2,1)} %bitcast.13), calls=%async_computation.1 | async-start | bytes 262144 | tf_op jit(solution)/shard_map/all_to_all | solution.py:210
  37.1 0.8 %copy-start.1 = (bf16[32,16,128]{2,1,0:T(8,128)(2,1)}, bf16[32,16,128]{2,1,0:T(8,128)(2,1)S(1)}, u32[]{:S(2)}) copy-start(bf16[32,16,128]{2,1,0:T(8,128)(2,1)S(1)} %all-to-all-done.1) | copy-start | bytes 393220

commit v2 on v1

v2 whole, which is shorter than its diff:
```python
import functools

import jax
import jax.numpy as jnp
from jax import lax
from jax.experimental import pallas as pl
from jax.experimental.pallas import tpu as pltpu
from jax.sharding import PartitionSpec as P

F32, BF16 = jnp.float32, jnp.bfloat16
VMEM_LIMIT = 24 * 1024 * 1024
FIRST_LIMIT = 60 * 1024 * 1024
BLOCK = 256
POWER, OFFSET = 20.75, 86.5
NN = (((1,), (0,)), ((), ()))
NT = (((1,), (1,)), ((), ()))


def dot(a, b, dims=NN):
    return lax.dot_general(a, b, dims, preferred_element_type=F32)


def halves(x):
    high = x.astype(BF16)
    return high, (x - high.astype(F32)).astype(BF16)


def dot3(a, b, dims=NN):
    ah, al = halves(a)
    bh, bl = halves(b)
    return dot(ah, bh, dims) + (dot(ah, bl, dims) + dot(al, bh, dims))


def encode(x):
    return jnp.exp(POWER * jnp.log(1.0 + 2.0 * x) - OFFSET).astype(BF16)


def decode(y):
    return 0.5 * jnp.exp((jnp.log(y.astype(F32)) + OFFSET) * (1.0 / POWER)) - 0.5


def in_hbm(x):
    return pltpu.with_memory_space_constraint(x, pltpu.HBM)


def forward_kernel(views, slices, bins, image_hbm, rx_hbm, ry_hbm, tof_hbm, out, image, rxt, ry, tof, rx, sems):
    first = pltpu.make_async_copy(tof_hbm, tof, sems.at[2 + slices])
    first.start()
    loads = [pltpu.make_async_copy(rx_hbm, rx, sems.at[0])]
    for z in range(slices):
        loads.append(pltpu.make_async_copy(image_hbm.at[z], image.at[z], sems.at[1 + z]))
    loads.append(pltpu.make_async_copy(ry_hbm, ry, sems.at[1 + slices]))
    for load in loads:
        load.start()
    rows = views * bins

    first.wait()
    loads[0].wait()
    pairs = [halves(dot(tof[v], rx[v])) for v in range(views)]
    weights = jnp.concatenate([p[0] for p in pairs] + [p[1] for p in pairs], axis=0)
    for v in range(views):
        rxt[v] = rx[v].T
    partial = []
    for z in range(slices):
        loads[1 + z].wait()
        both = dot(weights, image[z].astype(BF16))
        partial.append(both[:rows] + both[rows:])
    loads[1 + slices].wait()
    per_view = []
    for v in range(views):
        mine = jnp.concatenate([p[v * bins : (v + 1) * bins] for p in partial], axis=0)
        both = dot(jnp.concatenate(halves(mine), axis=0), ry[v])
        per_view.append(both[: slices * bins] + both[slices * bins :])
    joined = jnp.concatenate(
        [
            per_view[v][s * bins : (s + 1) * bins]
            for s in range(slices)
            for v in range(views)
        ],
        axis=0,
    )
    out[...] = encode(joined.T)


def swap_blocks(parts, width):
    n = len(parts)
    lane = lax.broadcasted_iota(jnp.int32, parts[0].shape, 1) // width
    step = 1
    while step < n:
        low = (lane // step) % 2 == 0
        new = list(parts)
        for i in range(n):
            if (i // step) % 2 == 0:
                a, b = parts[i], parts[i + step]
                shift = step * width
                new[i] = jnp.where(low, a, pltpu.roll(b, shift, 1))
                new[i + step] = jnp.where(
                    low, pltpu.roll(a, a.shape[1] - shift, 1), b
                )
        parts = new
        step *= 2
    return parts


def middle_kernel(views, slices, bins, owners, held, wire, mix, background, counts, out, turned, spread, sums_in):
    rows = views * bins
    lanes = slices * rows
    sums_in[...] = decode(wire[...])
    blocks = []
    for first in range(0, held, slices):
        parts = [
            sums_in[pl.ds(first + i, owners, stride=held), :] for i in range(slices)
        ]
        blocks.append(jnp.concatenate(swap_blocks(parts, rows), axis=0).T)
    for v in range(views):
        turned[...] = mix[v].T
        mixed = jnp.concatenate(
            [turned[pl.ds(s, owners, stride=slices), :] for s in range(slices)], axis=0
        )
        sums = jnp.concatenate(
            [
                blocks[j // slices][
                    (j % slices) * rows + v * bins : (j % slices) * rows + (v + 1) * bins
                ]
                for j in range(held)
            ],
            axis=0,
        )
        base = v * bins * held
        added = jnp.concatenate(
            [background[pl.ds(base + j, bins, stride=held), :] for j in range(held)], axis=0
        )
        seen = jnp.concatenate(
            [counts[pl.ds(base + j, bins, stride=held), :] for j in range(held)], axis=0
        )
        ratios = seen.astype(F32) / (added + dot3(sums, mixed))
        back = dot3(mixed, ratios, NT)
        groups = held * bins // lanes
        for s in range(slices):
            for g in range(groups):
                spread[pl.ds((s * views + v) * groups + g, owners, stride=slices * views * groups), :] = back[
                    s * owners : (s + 1) * owners, g * lanes : (g + 1) * lanes
                ]
    out[...] = spread[...].astype(BF16)


def corner(matrix, edge):
    near = matrix[edge - 8 : edge + 8, edge - 128 : edge + 128].astype(F32)
    row = lax.broadcasted_iota(jnp.int32, near.shape, 0) < 8
    column = lax.broadcasted_iota(jnp.int32, near.shape, 1) < 128
    return jnp.where(row != column, near, 0.0).astype(BF16)


def backward_kernel(views, slices, bins, owners, held, finish, *refs):
    if finish:
        wire, tof, ry, rxt, image, sensitivity_hbm, out_hbm = refs[:7]
    else:
        wire, tof, ry, rxt, out_hbm = refs[:5]
    result, wide, frames, unrotated, sensitivity, sems = refs[-6:]
    loads = []
    if finish:
        loads = [
            pltpu.make_async_copy(sensitivity_hbm.at[z], sensitivity.at[z], sems.at[image.shape[0] + z])
            for z in range(image.shape[0])
        ]
    for load in loads:
        load.start()
    cells = ry.shape[1]
    lanes = wire.shape[1]
    per_row = lanes // bins
    groups = held // per_row
    per_owner = slices * views * groups
    wide[...] = wire[...].astype(F32)
    mask = (
        lax.broadcasted_iota(jnp.int32, (per_row, lanes), 1) // bins
        == lax.broadcasted_iota(jnp.int32, (per_row, lanes), 0)
    )
    weights = [jnp.concatenate([tof[v]] * per_row, axis=0) for v in range(views)]
    for z in range(slices):
        for v in range(views):
            pieces = []
            for owner in range(owners):
                for g in range(groups):
                    row = owner * per_owner + (z * views + v) * groups + g
                    line = jnp.broadcast_to(wide[pl.ds(row, 1), :], (per_row, lanes))
                    pieces.append(jnp.where(mask, line, 0.0))
            back = jnp.concatenate(pieces, axis=0).astype(BF16)
            frames[z * views + v] = dot(back, weights[v]).astype(BF16)

    block = min(BLOCK, cells)
    edges = range(block, cells, block)
    ends = [[corner(ry[v], e)[:, 112:144] for e in edges] for v in range(views)]
    for i in range(slices * views):
        v = i % views
        for at in range(0, cells, block):
            own = dot(ry[v, at : at + block, at : at + block], frames[i, at : at + block, :])
            if at == 0:
                rows = [own]
            else:
                extra = dot(ends[v][at // block - 1], frames[i, at - 16 : at + 16, :])
                before, middle, after = rows[-1][:-8], rows[-1][-8:] + extra[:8], own[:8] + extra[8:]
                rows[-1] = jnp.concatenate([before, middle], axis=0)
                own = jnp.concatenate([after, own[8:]], axis=0)
                rows.append(own)
        for n, part in enumerate(rows):
            unrotated[i, n * block : (n + 1) * block, :] = part.astype(BF16)

    ends = [[corner(rxt[v], e) for e in edges] for v in range(views)]
    stores = []
    for z in range(slices):
        for at in range(0, cells, block):
            total = None
            for v in range(views):
                term = dot(
                    rxt[v, at : at + block, at : at + block],
                    unrotated[z * views + v, :, at : at + block],
                    NT,
                )
                total = term if total is None else total + term
            result[z, at : at + block, :] = total
        for n, e in enumerate(edges):
            total = None
            for v in range(views):
                term = dot(ends[v][n], unrotated[z * views + v, :, e - 128 : e + 128], NT)
                total = term if total is None else total + term
            result[z, e - 8 : e + 8, :] += total
        if finish:
            loads[z].wait()
            result[z] = image[z] * result[z] / sensitivity[z]
        store = pltpu.make_async_copy(result.at[z], out_hbm.at[z], sems.at[z])
        store.start()
        stores.append(store)
    for store in stores:
        store.wait()


def local(view_size, image, sensitivity, resample_x, resample_y, tof_kernel, axial_mix, background, counts):
    views, bins, cells = tof_kernel.shape
    slices, nx, ny = image.shape
    held, planes = background.shape[2:]
    owners = planes // slices
    lanes = slices * views * bins
    vmem = pl.BlockSpec(memory_space=pltpu.VMEM)
    anywhere = pl.BlockSpec(memory_space=pl.ANY)

    wire, current, rxt, ry, tof = pl.pallas_call(
        functools.partial(forward_kernel, views, slices, bins),
        in_specs=[anywhere] * 4,
        out_specs=[vmem] * 5,
        out_shape=[
            pltpu.VMEM((ny, lanes), BF16),
            pltpu.VMEM(image.shape, F32),
            pltpu.VMEM(resample_x.shape, BF16),
            pltpu.VMEM(resample_y.shape, BF16),
            pltpu.VMEM(tof_kernel.shape, BF16),
        ],
        scratch_shapes=[
            pltpu.VMEM(resample_x.shape, BF16),
            pltpu.SemaphoreType.DMA((3 + slices,)),
        ],
        compiler_params=pltpu.CompilerParams(vmem_limit_bytes=VMEM_LIMIT),
        name="project",
    )(*map(in_hbm, (image, resample_x, resample_y, tof_kernel)))
    wire = lax.all_to_all(
        wire.reshape(owners, held, lanes), "slab", 0, 0, tiled=True
    ).reshape(ny, lanes)

    per_owner = slices * views * (held * bins // lanes)
    back = pl.pallas_call(
        functools.partial(middle_kernel, views, slices, bins, owners, held),
        out_specs=vmem,
        out_shape=pltpu.VMEM((owners * per_owner, lanes), BF16),
        scratch_shapes=[
            pltpu.VMEM((planes, planes), F32),
            pltpu.VMEM((owners * per_owner, lanes), F32),
            pltpu.VMEM((owners * held, lanes), F32),
        ],
        compiler_params=pltpu.CompilerParams(vmem_limit_bytes=VMEM_LIMIT),
        name="compare",
    )(
        wire,
        axial_mix,
        background.reshape(-1, planes),
        counts.reshape(-1, planes),
    )
    back = lax.all_to_all(
        back.reshape(owners, per_owner, lanes), "slab", 0, 0, tiled=True
    ).reshape(owners * per_owner, lanes)

    finish = view_size == 1
    operands = [back, tof, ry, rxt]
    if finish:
        operands += [current, in_hbm(sensitivity)]
    stack = (slices * views, nx, ny)
    result = pl.pallas_call(
        functools.partial(backward_kernel, views, slices, bins, owners, held, finish),
        in_specs=[vmem] * 5 + [anywhere] if finish else [vmem] * 4,
        out_specs=anywhere,
        out_shape=jax.ShapeDtypeStruct((slices, nx, ny), F32),
        scratch_shapes=[
            pltpu.VMEM(image.shape, F32),
            pltpu.VMEM((owners * per_owner, lanes), F32),
            pltpu.VMEM(stack, BF16),
            pltpu.VMEM(stack, BF16),
            pltpu.VMEM(image.shape, F32),
            pltpu.SemaphoreType.DMA((2 * slices,)),
        ],
        compiler_params=pltpu.CompilerParams(vmem_limit_bytes=VMEM_LIMIT),
        name="backproject",
    )(*operands)
    if finish:
        return result
    gradient = lax.psum_scatter(result, "view", scatter_dimension=1, tiled=True)
    own_rows = nx // view_size
    own = lax.dynamic_slice_in_dim(image, lax.axis_index("view") * own_rows, own_rows, 1)
    return own * gradient / sensitivity


def solution(mesh):
    in_specs = (
        P("slab", None, None),
        P("slab", "view", None),
        P("view", None, None),
        P("view", None, None),
        P("view", None, None),
        P("view", None, None),
        P("view", None, "slab", None),
        P("view", None, "slab", None),
    )
    out_specs = P("slab", "view", None)
    return jax.shard_map(
        functools.partial(local, mesh.shape["view"]),
        mesh=mesh,
        in_specs=in_specs,
        out_specs=out_specs,
        check_vma=False,
    )
```

time: 48.8 us -> 36.3 us (0.74)
  Pallas kernels: 18.8 us -> 10.8 us
  blocking collectives: 18 us -> 25.3 us
  waiting for transfers between devices: 6.89 us -> 0 us
  starting transfers between devices: 2.58 us -> 0 us
  local copies, waits for them, and re-layouts: 2.1 us -> 0.01 us
    all_to_all x0 -> x1, blocking collectives: none -> 10 us  [local(): lax.all_to_all(back.reshape(owners, per_owner, lanes), 'slab', 0, 0, tile...]
    all_to_all x1 -> x0, waiting for transfers between devices: 6.89 us -> none  [local(): lax.all_to_all(back.reshape(owners, per_owner, lanes), 'slab', 0, 0, tile...]
    pallas_call x1, Pallas kernels: 10.5 us -> 6.41 us  [local(): pl.pallas_call(functools.partial(backward_kernel, views, slices, bins, ow...]
    all_to_all x1, blocking collectives: 18 us -> 15.3 us  [local(): lax.all_to_all(wire.reshape(owners, held, lanes), 'slab', 0, 0, tiled=True)]
    all_to_all x1 -> x0, starting transfers between devices: 2.58 us -> none  [local(): lax.all_to_all(back.reshape(owners, per_owner, lanes), 'slab', 0, 0, tile...]
    pallas_call x1, Pallas kernels: 5.51 us -> 3.39 us  [local(): pl.pallas_call(functools.partial(forward_kernel, views, slices, bins), in...]
    pallas_call x1, Pallas kernels: 2.75 us -> 1 us  [local(): pl.pallas_call(functools.partial(middle_kernel, views, slices, bins, owne...]
    unnamed x7 -> x6, local copies, waits for them, and re-layouts: 1.34 us -> 0.01 us
  transfers between devices with their start and end apart: 1 -> 0, of which waited for: 1 -> 0; matrix products, arithmetic and copies ran while one was open for 3% -> 0% of each run, Pallas kernels for 0% -> 0%
where the time goes in v2:
time: 36.3 us; the launch traced here: 36.2 us
  blocking collectives  25.3 us (70%)
  Pallas kernels  10.8 us (30%)
    all_to_all x1, blocking collectives, local(): lax.all_to_all(wire.reshape(owners, held, lanes), 'slab', 0, 0, tiled=True)  15.3 us
    all_to_all x1, blocking collectives, local(): lax.all_to_all(back.reshape(owners, per_owner, lanes), 'slab', 0, 0, tile...  10 us
    pallas_call x1, Pallas kernels, local(): pl.pallas_call(functools.partial(backward_kernel, views, slices, bins, ow...  6.41 us
    pallas_call x1, Pallas kernels, local(): pl.pallas_call(functools.partial(forward_kernel, views, slices, bins), in...  3.39 us
    pallas_call x1, Pallas kernels, local(): pl.pallas_call(functools.partial(middle_kernel, views, slices, bins, owne...  1 us

profile of v2, /device:TPU:0, one launch (start us, length us, event | category | flops | bytes accessed | tf_op | source)
XLA Modules:
  0.0 36.2 jit_solution(3004077609064188588)
XLA Ops:
  0.0 0.0 copy-start.1
  0.0 0.0 copy-start
  0.0 0.0 copy-start.2
  0.0 3.4 %project.1 = (bf16[512,128]{1,0:T(8,128)(2,1)S(1)}, f32[4,512,512]{2,1,0:T(8,128)S(1)}, bf16[2,512,512]{2,1,0:T(8,128)(2,1)S(1)}, bf16[2,512,512]{2,1,0:T(8,128)(2,1)S(1)}, bf16[2,16,512]{2,1,0:T(8,128)(2,1)S(1)}) custom-call(f32[4,512,512]{2,1,0:T(8,128)} %image_hbm.1, bf16[2,512,512]{2,1,0:T(8,128)(2,1)} %rx_hbm.1, bf16[2,512,512]{2,1,0:T(8,128)(2,1)} %ry_hbm.1, ...), custom_call_target="tpu_custom_call" | custom-call | tf_op jit(solution)/shard_map/project/pallas_call | solution.py:246
  3.4 15.3 %all_to_all.10 = bf16[32,16,128]{2,1,0:T(8,128)(2,1)S(1)} all-to-all(bf16[32,16,128]{2,1,0:T(8,128)(2,1)S(1)} %bitcast.11), channel_id=1, replica_groups=mesh['view'=1,'slab'=32] {'slab'}, dimensions={0} | all-to-all | bytes 262144 | tf_op jit(solution)/shard_map/all_to_all | solution.py:264
  18.7 0.0 copy-done.1
  18.7 0.0 copy-done
  18.7 0.0 copy-done.2
  18.8 1.0 %compare.1 = bf16[512,128]{1,0:T(8,128)(2,1)S(1)} custom-call(bf16[512,128]{1,0:T(8,128)(2,1)S(1)} %bitcast.7, f32[2,128,128]{2,1,0:T(8,128)S(1)} %copy-done.2, f32[512,128]{1,0:T(8,128)S(1)} %bitcast.9, s32[512,128]{1,0:T(8,128)S(1)} %bitcast.10), custom_call_target="tpu_custom_call" | custom-call | tf_op jit(solution)/shard_map/compare/pallas_call | solution.py:269
  19.8 10.0 %all_to_all.11 = bf16[32,16,128]{2,1,0:T(8,128)(2,1)S(1)} all-to-all(bf16[32,16,128]{2,1,0:T(8,128)(2,1)S(1)} %bitcast.8), channel_id=1, replica_groups=mesh['view'=1,'slab'=32] {'slab'}, dimensions={0} | all-to-all | bytes 262144 | tf_op jit(solution)/shard_map/all_to_all | solution.py:286
  29.8 6.4 %backproject.1 = f32[4,512,512]{2,1,0:T(8,128)} custom-call(bf16[512,128]{1,0:T(8,128)(2,1)S(1)} %bitcast.6, bf16[2,16,512]{2,1,0:T(8,128)(2,1)S(1)} %get-tuple-element.11.refs_1_, bf16[2,512,512]{2,1,0:T(8,128)(2,1)S(1)} %get-tuple-element.12.refs_2_, bf16[2,512,512]{2,1,0:T(8,128)(2,1)S(1)} %get-tuple-element.13.refs_3_, ...), custom_call_target="tpu_custom_call" | custom-call | tf_op jit(solution)/shard_map/backproject/pallas_call | solution.py:295
Async XLA Ops:
  0.0 18.7 %copy-start.1 = (s32[2,16,16,128]{3,2,1,0:T(8,128)S(1)}, s32[2,16,16,128]{3,2,1,0:T(8,128)}, u32[]{:S(2)}) copy-start(s32[2,16,16,128]{3,2,1,0:T(8,128)} %param.15) | copy-start | bytes 786436
  0.0 18.7 %copy-start = (f32[2,16,16,128]{3,2,1,0:T(8,128)S(1)}, f32[2,16,16,128]{3,2,1,0:T(8,128)}, u32[]{:S(2)}) copy-start(f32[2,16,16,128]{3,2,1,0:T(8,128)} %param.14) | copy-start | bytes 786436
  0.0 18.7 %copy-start.2 = (f32[2,128,128]{2,1,0:T(8,128)S(1)}, f32[2,128,128]{2,1,0:T(8,128)}, u32[]{:S(2)}) copy-start(f32[2,128,128]{2,1,0:T(8,128)} %mix.1) | copy-start | bytes 393220

commit v3 on v2

--- a/solution.py
+++ b/solution.py
@@ -10,7 +10,7 @@
 F32, BF16 = jnp.float32, jnp.bfloat16
 VMEM_LIMIT = 24 * 1024 * 1024
 FIRST_LIMIT = 60 * 1024 * 1024
-BLOCK = 256
+BLOCK, BAND, NEAR = 256, 3, 16
 POWER, OFFSET = 20.75, 86.5
 NN = (((1,), (0,)), ((), ()))
 NT = (((1,), (1,)), ((), ()))
@@ -43,33 +43,71 @@
     return pltpu.with_memory_space_constraint(x, pltpu.HBM)
 
 
-def forward_kernel(views, slices, bins, image_hbm, rx_hbm, ry_hbm, tof_hbm, out, image, rxt, ry, tof, rx, sems):
-    first = pltpu.make_async_copy(tof_hbm, tof, sems.at[2 + slices])
-    first.start()
-    loads = [pltpu.make_async_copy(rx_hbm, rx, sems.at[0])]
-    for z in range(slices):
-        loads.append(pltpu.make_async_copy(image_hbm.at[z], image.at[z], sems.at[1 + z]))
-    loads.append(pltpu.make_async_copy(ry_hbm, ry, sems.at[1 + slices]))
-    for load in loads:
+def banded(rows, matrix, edge):
+    cells = matrix.shape[0]
+    block = min(BLOCK, cells)
+    parts = [
+        dot(rows[:, at : at + block], matrix[at : at + block, at : at + block])
+        for at in range(0, cells, block)
+    ]
+    for n in range(1, len(parts)):
+        at = n * block
+        extra = dot(rows[:, at - NEAR : at + NEAR], corner(edge[n - 1]).astype(BF16))
+        parts[n - 1] = jnp.concatenate(
+            [parts[n - 1][:, : block - 128], parts[n - 1][:, block - 128 :] + extra[:, :128]], axis=1
+        )
+        parts[n] = jnp.concatenate([parts[n][:, :128] + extra[:, 128:], parts[n][:, 128:]], axis=1)
+    return jnp.concatenate(parts, axis=1)
+
+
+def forward_kernel(
+    views, slices, bins, image_hbm, rx_hbm, ry_hbm, tof_hbm,
+    out, image, rxt, ry, edge_y, edge_x, tof, rx, sems,
+):
+    cells = rx.shape[1]
+    block = min(BLOCK, cells)
+
+    def band_loads(source, target, edge, first):
+        copies = []
+        for at in range(0, cells, block):
+            place = (slice(None), pl.ds(at, block), pl.ds(at, block))
+            copies.append((source.at[place], target.at[place]))
+            if at > 0:
+                window = (slice(None), pl.ds(at - NEAR, 2 * NEAR), pl.ds(at - 128, 256))
+                copies.append((source.at[window], edge.at[:, at // block - 1]))
+        return [pltpu.make_async_copy(a, b, sems.at[first + n]) for n, (a, b) in enumerate(copies)]
+
+    per_band = 2 * (cells // block) - 1
+    load_tof = pltpu.make_async_copy(tof_hbm, tof, sems.at[0])
+    load_x = band_loads(rx_hbm, rx, edge_x, 1)
+    load_image = [
+        pltpu.make_async_copy(image_hbm.at[z], image.at[z], sems.at[1 + 2 * per_band + z])
+        for z in range(slices)
+    ]
+    load_y = band_loads(ry_hbm, ry, edge_y, 1 + per_band)
+    for load in [load_tof] + load_x + load_image + load_y:
         load.start()
     rows = views * bins
 
-    first.wait()
-    loads[0].wait()
-    pairs = [halves(dot(tof[v], rx[v])) for v in range(views)]
+    for load in [load_tof] + load_x:
+        load.wait()
+    pairs = [halves(banded(tof[v], rx.at[v], edge_x.at[v])) for v in range(views)]
     weights = jnp.concatenate([p[0] for p in pairs] + [p[1] for p in pairs], axis=0)
     for v in range(views):
-        rxt[v] = rx[v].T
+        for at in range(0, cells, block):
+            here = slice(at, at + block)
+            rxt[v, here, here] = rx[v, here, here].T
     partial = []
     for z in range(slices):
-        loads[1 + z].wait()
+        load_image[z].wait()
         both = dot(weights, image[z].astype(BF16))
         partial.append(both[:rows] + both[rows:])
-    loads[1 + slices].wait()
+    for load in load_y:
+        load.wait()
     per_view = []
     for v in range(views):
         mine = jnp.concatenate([p[v * bins : (v + 1) * bins] for p in partial], axis=0)
-        both = dot(jnp.concatenate(halves(mine), axis=0), ry[v])
+        both = banded(jnp.concatenate(halves(mine), axis=0), ry.at[v], edge_y.at[v])
         per_view.append(both[: slices * bins] + both[slices * bins :])
     joined = jnp.concatenate(
         [
@@ -144,27 +182,40 @@
     out[...] = spread[...].astype(BF16)
 
 
-def corner(matrix, edge):
-    near = matrix[edge - 8 : edge + 8, edge - 128 : edge + 128].astype(F32)
-    row = lax.broadcasted_iota(jnp.int32, near.shape, 0) < 8
-    column = lax.broadcasted_iota(jnp.int32, near.shape, 1) < 128
-    return jnp.where(row != column, near, 0.0).astype(BF16)
+def corner(window):
+    window = window.astype(F32)
+    row = lax.broadcasted_iota(jnp.int32, window.shape, 0) < window.shape[0] // 2
+    column = lax.broadcasted_iota(jnp.int32, window.shape, 1) < window.shape[1] // 2
+    return jnp.where(row != column, window, 0.0)
+
+
+def corner_columns(window, width):
+    near = corner(window)[NEAR - 8 : NEAR + 8]
+    spread = lambda rows, n: jnp.broadcast_to(near[rows, n : n + 1], (8, width))
+    return (
+        [spread(slice(0, 8), 128 + n) for n in range(BAND)],
+        [spread(slice(8, 16), 127 - n) for n in range(BAND)],
+    )
+
+
+def corner_rows(window, width):
+    near = corner(window)[:, 120:136]
+    flat = jnp.concatenate([near, jnp.zeros((2 * NEAR, 112), F32)], axis=1)
+    turned = jnp.concatenate([flat, jnp.zeros((128 - 2 * NEAR, 128), F32)], axis=0).T
+    spread = lambda rows, n: jnp.broadcast_to(turned[rows, n : n + 1], (8, width))
+    return (
+        [spread(slice(0, 8), NEAR + n) for n in range(BAND)],
+        [spread(slice(8, 16), NEAR - 1 - n) for n in range(BAND)],
+    )
 
 
 def backward_kernel(views, slices, bins, owners, held, finish, *refs):
     if finish:
-        wire, tof, ry, rxt, image, sensitivity_hbm, out_hbm = refs[:7]
+        wire, tof, ry, rxt, edge_y, edge_x, image, sensitivity, out_hbm = refs[:9]
     else:
-        wire, tof, ry, rxt, out_hbm = refs[:5]
-    result, wide, frames, unrotated, sensitivity, sems = refs[-6:]
-    loads = []
-    if finish:
-        loads = [
-            pltpu.make_async_copy(sensitivity_hbm.at[z], sensitivity.at[z], sems.at[image.shape[0] + z])
-            for z in range(image.shape[0])
-        ]
-    for load in loads:
-        load.start()
+        wire, tof, ry, rxt, edge_y, edge_x, out_hbm = refs[:7]
+    result, wide, frames, unrotated, packed, sides, sems = refs[-7:]
+
     cells = ry.shape[1]
     lanes = wire.shape[1]
     per_row = lanes // bins
@@ -176,7 +227,13 @@
         == lax.broadcasted_iota(jnp.int32, (per_row, lanes), 0)
     )
     weights = [jnp.concatenate([tof[v]] * per_row, axis=0) for v in range(views)]
-    for z in range(slices):
+    block = min(BLOCK, cells)
+    edges = range(block, cells, block)
+    ends_y = [[corner_columns(edge_y[v, n], cells) for n in range(len(edges))] for v in range(views)]
+    ends_x = [[corner_rows(edge_x[v, n], cells) for n in range(len(edges))] for v in range(views)]
+    stores = []
+
+    def spread_frames(z):
         for v in range(views):
             pieces = []
             for owner in range(owners):
@@ -187,27 +244,36 @@
             back = jnp.concatenate(pieces, axis=0).astype(BF16)
             frames[z * views + v] = dot(back, weights[v]).astype(BF16)
 
-    block = min(BLOCK, cells)
-    edges = range(block, cells, block)
-    ends = [[corner(ry[v], e)[:, 112:144] for e in edges] for v in range(views)]
-    for i in range(slices * views):
-        v = i % views
-        for at in range(0, cells, block):
-            own = dot(ry[v, at : at + block, at : at + block], frames[i, at : at + block, :])
-            if at == 0:
-                rows = [own]
-            else:
-                extra = dot(ends[v][at // block - 1], frames[i, at - 16 : at + 16, :])
-                before, middle, after = rows[-1][:-8], rows[-1][-8:] + extra[:8], own[:8] + extra[8:]
-                rows[-1] = jnp.concatenate([before, middle], axis=0)
-                own = jnp.concatenate([after, own[8:]], axis=0)
+    def unrotate(z):
+        for v in range(views):
+            i = z * views + v
+            rows = []
+            for at in range(0, cells, block):
+                own = dot(ry[v, at : at + block, at : at + block], frames[i, at : at + block, :])
+                if at > 0:
+                    above, below = ends_y[v][at // block - 1]
+                    near = frames[i, at - 16 : at + 16, :].astype(F32)
+                    last, first = rows[-1][-8:], own[:8]
+                    for n in range(BAND):
+                        last += above[n] * near[16 + n : 17 + n]
+                        first += below[n] * near[15 - n : 16 - n]
+                    rows[-1] = jnp.concatenate([rows[-1][:-8], last], axis=0)
+                    own = jnp.concatenate([first, own[8:]], axis=0)
                 rows.append(own)
-        for n, part in enumerate(rows):
-            unrotated[i, n * block : (n + 1) * block, :] = part.astype(BF16)
-
-    ends = [[corner(rxt[v], e) for e in edges] for v in range(views)]
-    stores = []
-    for z in range(slices):
+            for n, part in enumerate(rows):
+                here = slice(n * block, (n + 1) * block)
+                part = part.astype(BF16)
+                unrotated[i, here, :] = part
+                for m, e in enumerate(edges):
+                    left = part[:, e - 128 : e].astype(F32)
+                    right = part[:, e : e + 128].astype(F32)
+                    lane = lax.broadcasted_iota(jnp.int32, left.shape, 1)
+                    spot = 16 * (i % (half * views))
+                    around = pltpu.roll(jnp.where(lane < 64, right, left), (spot + 8) % 128, 1)
+                    packed[z // half, m, here, spot : spot + 16] = around[:, spot : spot + 16]
+
+    def finish_slice(z):
+        strips = []
         for at in range(0, cells, block):
             total = None
             for v in range(views):
@@ -217,19 +283,36 @@
                     NT,
                 )
                 total = term if total is None else total + term
-            result[z, at : at + block, :] = total
-        for n, e in enumerate(edges):
-            total = None
-            for v in range(views):
-                term = dot(ends[v][n], unrotated[z * views + v, :, e - 128 : e + 128], NT)
-                total = term if total is None else total + term
-            result[z, e - 8 : e + 8, :] += total
-        if finish:
-            loads[z].wait()
-            result[z] = image[z] * result[z] / sensitivity[z]
+            if at > 0:
+                last, first = strips[-1][-8:], total[:8]
+                for v in range(views):
+                    above, below = ends_x[v][at // block - 1]
+                    own = (z % half * views + v) * 16
+                    for n in range(BAND):
+                        last += above[n] * sides[z // half, at // block - 1, pl.ds(own + 8 + n, 1), :]
+                        first += below[n] * sides[z // half, at // block - 1, pl.ds(own + 7 - n, 1), :]
+                strips[-1] = jnp.concatenate([strips[-1][:-8], last], axis=0)
+                total = jnp.concatenate([first, total[8:]], axis=0)
+            strips.append(total)
+        for n, strip in enumerate(strips):
+            rows = pl.ds(n * block, block)
+            if finish:
+                strip = image[z, rows, :] * strip / sensitivity[z, rows, :]
+            result[z, rows, :] = strip
         store = pltpu.make_async_copy(result.at[z], out_hbm.at[z], sems.at[z])
         store.start()
         stores.append(store)
+
+    half = 1
+    for z in range(slices):
+        spread_frames(z)
+    for z in range(slices + 1):
+        if z < slices:
+            unrotate(z)
+            for m in range(len(edges)):
+                sides[z, m] = packed[z, m].T
+        if z > 0:
+            finish_slice(z - 1)
     for store in stores:
         store.wait()
 
@@ -243,20 +326,24 @@
     vmem = pl.BlockSpec(memory_space=pltpu.VMEM)
     anywhere = pl.BlockSpec(memory_space=pl.ANY)
 
-    wire, current, rxt, ry, tof = pl.pallas_call(
+    block = min(BLOCK, nx)
+    edge_shape = (views, max(nx // block - 1, 1), 2 * NEAR, 256)
+    wire, current, rxt, ry, edge_y, edge_x, tof = pl.pallas_call(
         functools.partial(forward_kernel, views, slices, bins),
         in_specs=[anywhere] * 4,
-        out_specs=[vmem] * 5,
+        out_specs=[vmem] * 7,
         out_shape=[
             pltpu.VMEM((ny, lanes), BF16),
             pltpu.VMEM(image.shape, F32),
             pltpu.VMEM(resample_x.shape, BF16),
             pltpu.VMEM(resample_y.shape, BF16),
+            pltpu.VMEM(edge_shape, BF16),
+            pltpu.VMEM(edge_shape, BF16),
             pltpu.VMEM(tof_kernel.shape, BF16),
         ],
         scratch_shapes=[
             pltpu.VMEM(resample_x.shape, BF16),
-            pltpu.SemaphoreType.DMA((3 + slices,)),
+            pltpu.SemaphoreType.DMA((1 + 2 * (2 * (nx // block) - 1) + slices,)),
         ],
         compiler_params=pltpu.CompilerParams(vmem_limit_bytes=VMEM_LIMIT),
         name="project",
@@ -276,6 +363,7 @@
             pltpu.VMEM((owners * held, lanes), F32),
         ],
         compiler_params=pltpu.CompilerParams(vmem_limit_bytes=VMEM_LIMIT),
+        cost_estimate=pl.CostEstimate(flops=0, bytes_accessed=40 * 1024 * 1024, transcendentals=0),
         name="compare",
     )(
         wire,
@@ -288,13 +376,13 @@
     ).reshape(owners * per_owner, lanes)
 
     finish = view_size == 1
-    operands = [back, tof, ry, rxt]
+    operands = [back, tof, ry, rxt, edge_y, edge_x]
     if finish:
-        operands += [current, in_hbm(sensitivity)]
+        operands += [current, sensitivity]
     stack = (slices * views, nx, ny)
     result = pl.pallas_call(
         functools.partial(backward_kernel, views, slices, bins, owners, held, finish),
-        in_specs=[vmem] * 5 + [anywhere] if finish else [vmem] * 4,
+        in_specs=[vmem] * len(operands),
         out_specs=anywhere,
         out_shape=jax.ShapeDtypeStruct((slices, nx, ny), F32),
         scratch_shapes=[
@@ -302,8 +390,9 @@
             pltpu.VMEM((owners * per_owner, lanes), F32),
             pltpu.VMEM(stack, BF16),
             pltpu.VMEM(stack, BF16),
-            pltpu.VMEM(image.shape, F32),
-            pltpu.SemaphoreType.DMA((2 * slices,)),
+            pltpu.VMEM((slices, pl.cdiv(nx, BLOCK), ny, 16 * views), F32),
+            pltpu.VMEM((slices, pl.cdiv(nx, BLOCK), 16 * views, ny), F32),
+            pltpu.SemaphoreType.DMA((slices,)),
         ],
         compiler_params=pltpu.CompilerParams(vmem_limit_bytes=VMEM_LIMIT),
         name="backproject",

time: 36.3 us -> 34.4 us (0.948)
  Pallas kernels: 10.8 us -> 8.84 us
    pallas_call x1, Pallas kernels: 6.41 us -> 4.6 us  [local(): pl.pallas_call(functools.partial(backward_kernel, views, slices, bins, ow...]
where the time goes in v3:
time: 34.4 us; the launch traced here: 34.2 us
  blocking collectives  25.4 us (74%)
  Pallas kernels  8.84 us (26%)
    all_to_all x1, blocking collectives, local(): lax.all_to_all(wire.reshape(owners, held, lanes), 'slab', 0, 0, tiled=True)  15.3 us
    all_to_all x1, blocking collectives, local(): lax.all_to_all(back.reshape(owners, per_owner, lanes), 'slab', 0, 0, tile...  10 us
    pallas_call x1, Pallas kernels, local(): pl.pallas_call(functools.partial(backward_kernel, views, slices, bins, ow...  4.6 us
    pallas_call x1, Pallas kernels, local(): pl.pallas_call(functools.partial(forward_kernel, views, slices, bins), in...  3.25 us
    pallas_call x1, Pallas kernels, local(): pl.pallas_call(functools.partial(middle_kernel, views, slices, bins, owne...  1 us

profile of v3, /device:TPU:0, one launch (start us, length us, event | category | flops | bytes accessed | tf_op | source)
XLA Modules:
  0.0 34.2 jit_solution(10727116381220486210)
XLA Ops:
  0.0 0.0 copy-start.2
  0.0 0.0 copy-start.1
  0.0 0.0 copy-start.3
  0.0 0.0 copy-start
  0.0 3.2 %project.1 = (bf16[512,128]{1,0:T(8,128)(2,1)S(1)}, f32[4,512,512]{2,1,0:T(8,128)S(1)}, bf16[2,512,512]{2,1,0:T(8,128)(2,1)S(1)}, bf16[2,512,512]{2,1,0:T(8,128)...) custom-call(f32[4,512,512]{2,1,0:T(8,128)} %image_hbm.1, ...), custom_call_target="tpu_custom_call" | custom-call | tf_op jit(solution)/shard_map/project/pallas_call | solution.py:331
  3.3 15.3 %all_to_all.10 = bf16[32,16,128]{2,1,0:T(8,128)(2,1)S(1)} all-to-all(bf16[32,16,128]{2,1,0:T(8,128)(2,1)S(1)} %bitcast.11), channel_id=1, replica_groups=mesh['view'=1,'slab'=32] {'slab'}, dimensions={0} | all-to-all | bytes 262144 | tf_op jit(solution)/shard_map/all_to_all | solution.py:351
  18.6 0.0 copy-done.2
  18.6 0.0 copy-done.1
  18.6 0.0 copy-done.3
  18.6 1.0 %compare.1 = bf16[512,128]{1,0:T(8,128)(2,1)S(1)} custom-call(bf16[512,128]{1,0:T(8,128)(2,1)S(1)} %bitcast.7, f32[2,128,128]{2,1,0:T(8,128)S(1)} %copy-done.3, f32[512,128]{1,0:T(8,128)S(1)} %bitcast.9, s32[512,128]{1,0:T(8,128)S(1)} %bitcast.10), custom_call_target="tpu_custom_call" | custom-call | bytes 41943040 | tf_op jit(solution)/shard_map/compare/pallas_call | solution.py:356
  19.6 10.0 %all_to_all.11 = bf16[32,16,128]{2,1,0:T(8,128)(2,1)S(1)} all-to-all(bf16[32,16,128]{2,1,0:T(8,128)(2,1)S(1)} %bitcast.8), channel_id=1, replica_groups=mesh['view'=1,'slab'=32] {'slab'}, dimensions={0} | all-to-all | bytes 262144 | tf_op jit(solution)/shard_map/all_to_all | solution.py:374
  29.6 0.0 copy-done
  29.6 4.6 %backproject.1 = f32[4,512,512]{2,1,0:T(8,128)} custom-call(bf16[512,128]{1,0:T(8,128)(2,1)S(1)} %bitcast.6, bf16[2,16,512]{2,1,0:T(8,128)(2,1)S(1)} %get-tuple-element.13.refs_1_, bf16[2,512,512]{2,1,0:T(8,128)(2,1)S(1)} %get-tuple-element.14.refs_2_, bf16[2,512,512]{2,1,0:T(8,128)(2,1)S(1)} %get-tuple-element.15.refs_3_, ...), custom_call_target="tpu_custom_call" | custom-call | tf_op jit(solution)/shard_map/backproject/pallas_call | solution.py:383
Async XLA Ops:
  0.0 18.6 %copy-start.2 = (s32[2,16,16,128]{3,2,1,0:T(8,128)S(1)}, s32[2,16,16,128]{3,2,1,0:T(8,128)}, u32[]{:S(2)}) copy-start(s32[2,16,16,128]{3,2,1,0:T(8,128)} %param.15) | copy-start | bytes 786436
  0.0 18.6 %copy-start.1 = (f32[2,16,16,128]{3,2,1,0:T(8,128)S(1)}, f32[2,16,16,128]{3,2,1,0:T(8,128)}, u32[]{:S(2)}) copy-start(f32[2,16,16,128]{3,2,1,0:T(8,128)} %param.14) | copy-start | bytes 786436
  0.0 18.6 %copy-start.3 = (f32[2,128,128]{2,1,0:T(8,128)S(1)}, f32[2,128,128]{2,1,0:T(8,128)}, u32[]{:S(2)}) copy-start(f32[2,128,128]{2,1,0:T(8,128)} %mix.1) | copy-start | bytes 393220
  0.0 29.6 %copy-start = (f32[4,512,512]{2,1,0:T(8,128)S(1)}, f32[4,512,512]{2,1,0:T(8,128)}, u32[]{:S(2)}) copy-start(f32[4,512,512]{2,1,0:T(8,128)} %refs_7_.1) | copy-start | bytes 12582916

commit v4 on v3

--- a/solution.py
+++ b/solution.py
@@ -10,7 +10,7 @@
 F32, BF16 = jnp.float32, jnp.bfloat16
 VMEM_LIMIT = 24 * 1024 * 1024
 FIRST_LIMIT = 60 * 1024 * 1024
-BLOCK, BAND, NEAR = 256, 3, 16
+BLOCK, NARROW, BAND, NEAR = 256, 128, 3, 16
 POWER, OFFSET = 20.75, 86.5
 NN = (((1,), (0,)), ((), ()))
 NT = (((1,), (1,)), ((), ()))
@@ -43,7 +43,7 @@
     return pltpu.with_memory_space_constraint(x, pltpu.HBM)
 
 
-def banded(rows, matrix, edge):
+def banded(rows, matrix, edge, between=1):
     cells = matrix.shape[0]
     block = min(BLOCK, cells)
     parts = [
@@ -52,7 +52,7 @@
     ]
     for n in range(1, len(parts)):
         at = n * block
-        extra = dot(rows[:, at - NEAR : at + NEAR], corner(edge[n - 1]).astype(BF16))
+        extra = dot(rows[:, at - NEAR : at + NEAR], corner(edge[n * between - 1]).astype(BF16))
         parts[n - 1] = jnp.concatenate(
             [parts[n - 1][:, : block - 128], parts[n - 1][:, block - 128 :] + extra[:, :128]], axis=1
         )
@@ -62,48 +62,64 @@
 
 def forward_kernel(
     views, slices, bins, image_hbm, rx_hbm, ry_hbm, tof_hbm,
-    out, image, rxt, ry, edge_y, edge_x, tof, rx, sems,
+    out, image, strips_x, ryt, edge_y, edge_x, toft, tof, rx, ry, sems,
 ):
     cells = rx.shape[1]
     block = min(BLOCK, cells)
 
-    def band_loads(source, target, edge, first):
+    def band(source, target, edge, step):
         copies = []
         for at in range(0, cells, block):
             place = (slice(None), pl.ds(at, block), pl.ds(at, block))
             copies.append((source.at[place], target.at[place]))
             if at > 0:
                 window = (slice(None), pl.ds(at - NEAR, 2 * NEAR), pl.ds(at - 128, 256))
-                copies.append((source.at[window], edge.at[:, at // block - 1]))
-        return [pltpu.make_async_copy(a, b, sems.at[first + n]) for n, (a, b) in enumerate(copies)]
-
-    per_band = 2 * (cells // block) - 1
-    load_tof = pltpu.make_async_copy(tof_hbm, tof, sems.at[0])
-    load_x = band_loads(rx_hbm, rx, edge_x, 1)
-    load_image = [
-        pltpu.make_async_copy(image_hbm.at[z], image.at[z], sems.at[1 + 2 * per_band + z])
-        for z in range(slices)
-    ]
-    load_y = band_loads(ry_hbm, ry, edge_y, 1 + per_band)
-    for load in [load_tof] + load_x + load_image + load_y:
+                copies.append((source.at[window], edge.at[:, at // step - 1]))
+        return copies
+
+    images = [(image_hbm.at[z], image.at[z]) for z in range(slices)]
+    groups = [[(tof_hbm, tof)] + band(rx_hbm, rx, edge_x, NARROW)]
+    groups += [images[:1], images[1:2], band(ry_hbm, ry, edge_y, block)]
+    groups += [[pair] for pair in images[2:]]
+    loads, n = [], 0
+    for group in groups:
+        loads.append([pltpu.make_async_copy(*pair, sems.at[n + i]) for i, pair in enumerate(group)])
+        n += len(group)
+    for load in sum(loads, []):
         load.start()
+    loads = iter(loads)
+
+    def arrive():
+        for load in next(loads):
+            load.wait()
+
     rows = views * bins
-
-    for load in [load_tof] + load_x:
-        load.wait()
-    pairs = [halves(banded(tof[v], rx.at[v], edge_x.at[v])) for v in range(views)]
+    per_row = toft.shape[2] // bins
+    partial = []
+
+    def add_slice(z):
+        arrive()
+        both = dot(weights, image[z].astype(BF16))
+        partial.append(both[:rows] + both[rows:])
+
+    arrive()
+    pairs = [halves(banded(tof[v], rx.at[v], edge_x.at[v], block // NARROW)) for v in range(views)]
     weights = jnp.concatenate([p[0] for p in pairs] + [p[1] for p in pairs], axis=0)
+    add_slice(0)
     for v in range(views):
+        for n, at in enumerate(range(0, cells, NARROW)):
+            strips_x[n, :, v * NARROW : (v + 1) * NARROW] = rx[v, at : at + NARROW, at : at + NARROW].T
+            if at % block > 0:
+                edge_x[v, n - 1] = rx[v, at - NEAR : at + NEAR, at - 128 : at + 128]
+    add_slice(1)
+    arrive()
+    for v in range(views):
+        toft[v] = jnp.concatenate([tof[v]] * per_row, axis=0).T
         for at in range(0, cells, block):
             here = slice(at, at + block)
-            rxt[v, here, here] = rx[v, here, here].T
-    partial = []
-    for z in range(slices):
-        load_image[z].wait()
-        both = dot(weights, image[z].astype(BF16))
-        partial.append(both[:rows] + both[rows:])
-    for load in load_y:
-        load.wait()
+            ryt[v, here, here] = ry[v, here, here].T
+    for z in range(2, slices):
+        add_slice(z)
     per_view = []
     for v in range(views):
         mine = jnp.concatenate([p[v * bins : (v + 1) * bins] for p in partial], axis=0)
@@ -210,13 +226,12 @@
 
 
 def backward_kernel(views, slices, bins, owners, held, finish, *refs):
+    wire, tof, toft, ryt, strips_x, edge_y, edge_x = refs[:7]
     if finish:
-        wire, tof, ry, rxt, edge_y, edge_x, image, sensitivity, out_hbm = refs[:9]
-    else:
-        wire, tof, ry, rxt, edge_y, edge_x, out_hbm = refs[:7]
-    result, wide, frames, unrotated, packed, sides, sems = refs[-7:]
-
-    cells = ry.shape[1]
+        image, sensitivity = refs[7:9]
+    out_hbm, result, wide, frames, unrotated, turned, sems = refs[-7:]
+
+    cells = ryt.shape[1]
     lanes = wire.shape[1]
     per_row = lanes // bins
     groups = held // per_row
@@ -226,93 +241,96 @@
         lax.broadcasted_iota(jnp.int32, (per_row, lanes), 1) // bins
         == lax.broadcasted_iota(jnp.int32, (per_row, lanes), 0)
     )
-    weights = [jnp.concatenate([tof[v]] * per_row, axis=0) for v in range(views)]
     block = min(BLOCK, cells)
     edges = range(block, cells, block)
-    ends_y = [[corner_columns(edge_y[v, n], cells) for n in range(len(edges))] for v in range(views)]
-    ends_x = [[corner_rows(edge_x[v, n], cells) for n in range(len(edges))] for v in range(views)]
+    narrow_edges = range(NARROW, cells, NARROW)
+    ends_x = [[corner_rows(edge_x[v, n], cells) for n in range(len(narrow_edges))] for v in range(views)]
     stores = []
+
+    def line(z, v, first):
+        row = first // held * per_owner + (z * views + v) * groups + first % held // per_row
+        return jnp.where(mask, jnp.broadcast_to(wide[pl.ds(row, 1), :], (per_row, lanes)), 0.0)
 
     def spread_frames(z):
         for v in range(views):
-            pieces = []
-            for owner in range(owners):
-                for g in range(groups):
-                    row = owner * per_owner + (z * views + v) * groups + g
-                    line = jnp.broadcast_to(wide[pl.ds(row, 1), :], (per_row, lanes))
-                    pieces.append(jnp.where(mask, line, 0.0))
-            back = jnp.concatenate(pieces, axis=0).astype(BF16)
-            frames[z * views + v] = dot(back, weights[v]).astype(BF16)
+            back = jnp.concatenate([line(z, v, n) for n in range(0, cells, per_row)], axis=0)
+            frames[z * views + v] = dot(toft[v], back.astype(BF16), NT).astype(BF16)
+
+    def edge_frames(n, edge):
+        extra = []
+        for v in range(views):
+            near = [line(z, v, first) for z in range(slices) for first in (edge - 8, edge)]
+            weights = jnp.concatenate([tof[v]] * per_row, axis=0)
+            near = dot(jnp.concatenate(near, axis=0).astype(BF16), weights).astype(BF16).astype(F32)
+            above, below = corner_columns(edge_y[v, n], cells)
+            for z in range(slices):
+                own = near[16 * z : 16 * z + 16]
+                extra.append(sum(above[m] * own[8 + m : 9 + m] for m in range(BAND)))
+                extra.append(sum(below[m] * own[7 - m : 8 - m] for m in range(BAND)))
+        turned[n] = jnp.concatenate(extra, axis=0).T
 
     def unrotate(z):
         for v in range(views):
             i = z * views + v
-            rows = []
-            for at in range(0, cells, block):
-                own = dot(ry[v, at : at + block, at : at + block], frames[i, at : at + block, :])
-                if at > 0:
-                    above, below = ends_y[v][at // block - 1]
-                    near = frames[i, at - 16 : at + 16, :].astype(F32)
-                    last, first = rows[-1][-8:], own[:8]
-                    for n in range(BAND):
-                        last += above[n] * near[16 + n : 17 + n]
-                        first += below[n] * near[15 - n : 16 - n]
-                    rows[-1] = jnp.concatenate([rows[-1][:-8], last], axis=0)
-                    own = jnp.concatenate([first, own[8:]], axis=0)
-                rows.append(own)
-            for n, part in enumerate(rows):
-                here = slice(n * block, (n + 1) * block)
+            parts = [
+                dot(frames[i, :, at : at + block], ryt[v, at : at + block, at : at + block])
+                for at in range(0, cells, block)
+            ]
+            for n in range(len(edges)):
+                extra = turned[n]
+                lane = lax.broadcasted_iota(jnp.int32, extra.shape, 1)
+                extra = pltpu.roll(extra, (120 - 16 * (v * slices + z)) % 128, 1)
+                left, right = parts[n], parts[n + 1]
+                parts[n] = jnp.concatenate(
+                    [left[:, :-128], left[:, -128:] + jnp.where(lane >= 120, extra, 0.0)], axis=1
+                )
+                parts[n + 1] = jnp.concatenate(
+                    [right[:, :128] + jnp.where(lane < 8, extra, 0.0), right[:, 128:]], axis=1
+                )
+            for n, part in enumerate(parts):
                 part = part.astype(BF16)
-                unrotated[i, here, :] = part
-                for m, e in enumerate(edges):
-                    left = part[:, e - 128 : e].astype(F32)
-                    right = part[:, e : e + 128].astype(F32)
-                    lane = lax.broadcasted_iota(jnp.int32, left.shape, 1)
-                    spot = 16 * (i % (half * views))
-                    around = pltpu.roll(jnp.where(lane < 64, right, left), (spot + 8) % 128, 1)
-                    packed[z // half, m, here, spot : spot + 16] = around[:, spot : spot + 16]
+                for w in range(cells // NARROW):
+                    unrotated[z, w, v * NARROW : (v + 1) * NARROW, n * block : (n + 1) * block] = part[
+                        w * NARROW : (w + 1) * NARROW
+                    ]
 
     def finish_slice(z):
-        strips = []
-        for at in range(0, cells, block):
-            total = None
+        for w in range(cells // NARROW):
+            part = dot(strips_x[w], unrotated[z, w])
+            first, last = part[:8], part[-8:]
             for v in range(views):
-                term = dot(
-                    rxt[v, at : at + block, at : at + block],
-                    unrotated[z * views + v, :, at : at + block],
-                    NT,
-                )
-                total = term if total is None else total + term
-            if at > 0:
-                last, first = strips[-1][-8:], total[:8]
-                for v in range(views):
-                    above, below = ends_x[v][at // block - 1]
-                    own = (z % half * views + v) * 16
-                    for n in range(BAND):
-                        last += above[n] * sides[z // half, at // block - 1, pl.ds(own + 8 + n, 1), :]
-                        first += below[n] * sides[z // half, at // block - 1, pl.ds(own + 7 - n, 1), :]
-                strips[-1] = jnp.concatenate([strips[-1][:-8], last], axis=0)
-                total = jnp.concatenate([first, total[8:]], axis=0)
-            strips.append(total)
-        for n, strip in enumerate(strips):
-            rows = pl.ds(n * block, block)
+                if w > 0:
+                    end = (v + 1) * NARROW
+                    near = unrotated[z, w - 1, end - 16 : end, :].astype(F32)
+                    for m in range(BAND):
+                        first += ends_x[v][w - 1][1][m] * near[15 - m : 16 - m]
+                if (w + 1) * NARROW < cells:
+                    near = unrotated[z, w + 1, v * NARROW : v * NARROW + 16, :].astype(F32)
+                    for m in range(BAND):
+                        last += ends_x[v][w][0][m] * near[m : m + 1]
+            part = jnp.concatenate([first, part[8:-8], last], axis=0)
+            rows = slice(w * NARROW, (w + 1) * NARROW)
             if finish:
-                strip = image[z, rows, :] * strip / sensitivity[z, rows, :]
-            result[z, rows, :] = strip
-        store = pltpu.make_async_copy(result.at[z], out_hbm.at[z], sems.at[z])
+                part = image[z, rows, :] * part / sensitivity[z, rows, :]
+            result[z, rows, :] = part
+            if z == slices - 1:
+                keep(result.at[z, rows], out_hbm.at[z, rows])
+        if z < slices - 1:
+            keep(result.at[z], out_hbm.at[z])
+
+    def keep(source, target):
+        store = pltpu.make_async_copy(source, target, sems.at[len(stores)])
         store.start()
         stores.append(store)
 
-    half = 1
+    spread_frames(0)
+    for n, edge in enumerate(edges):
+        edge_frames(n, edge)
     for z in range(slices):
-        spread_frames(z)
-    for z in range(slices + 1):
-        if z < slices:
-            unrotate(z)
-            for m in range(len(edges)):
-                sides[z, m] = packed[z, m].T
-        if z > 0:
-            finish_slice(z - 1)
+        unrotate(z)
+        if z + 1 < slices:
+            spread_frames(z + 1)
+        finish_slice(z)
     for store in stores:
         store.wait()
 
@@ -327,23 +345,25 @@
     anywhere = pl.BlockSpec(memory_space=pl.ANY)
 
     block = min(BLOCK, nx)
-    edge_shape = (views, max(nx // block - 1, 1), 2 * NEAR, 256)
-    wire, current, rxt, ry, edge_y, edge_x, tof = pl.pallas_call(
+    narrow = nx // NARROW
+    wire, current, strips_x, ryt, edge_y, edge_x, toft, tof = pl.pallas_call(
         functools.partial(forward_kernel, views, slices, bins),
         in_specs=[anywhere] * 4,
-        out_specs=[vmem] * 7,
+        out_specs=[vmem] * 8,
         out_shape=[
             pltpu.VMEM((ny, lanes), BF16),
             pltpu.VMEM(image.shape, F32),
-            pltpu.VMEM(resample_x.shape, BF16),
+            pltpu.VMEM((narrow, NARROW, views * NARROW), BF16),
             pltpu.VMEM(resample_y.shape, BF16),
-            pltpu.VMEM(edge_shape, BF16),
-            pltpu.VMEM(edge_shape, BF16),
+            pltpu.VMEM((views, max(ny // block - 1, 1), 2 * NEAR, 256), BF16),
+            pltpu.VMEM((views, max(narrow - 1, 1), 2 * NEAR, 256), BF16),
+            pltpu.VMEM((views, nx, lanes), BF16),
             pltpu.VMEM(tof_kernel.shape, BF16),
         ],
         scratch_shapes=[
             pltpu.VMEM(resample_x.shape, BF16),
-            pltpu.SemaphoreType.DMA((1 + 2 * (2 * (nx // block) - 1) + slices,)),
+            pltpu.VMEM(resample_y.shape, BF16),
+            pltpu.SemaphoreType.DMA((4 * (nx // block) - 1 + slices,)),
         ],
         compiler_params=pltpu.CompilerParams(vmem_limit_bytes=VMEM_LIMIT),
         name="project",
@@ -376,10 +396,9 @@
     ).reshape(owners * per_owner, lanes)
 
     finish = view_size == 1
-    operands = [back, tof, ry, rxt, edge_y, edge_x]
+    operands = [back, tof, toft, ryt, strips_x, edge_y, edge_x]
     if finish:
         operands += [current, sensitivity]
-    stack = (slices * views, nx, ny)
     result = pl.pallas_call(
         functools.partial(backward_kernel, views, slices, bins, owners, held, finish),
         in_specs=[vmem] * len(operands),
@@ -388,11 +407,10 @@
         scratch_shapes=[
             pltpu.VMEM(image.shape, F32),
             pltpu.VMEM((owners * per_owner, lanes), F32),
-            pltpu.VMEM(stack, BF16),
-            pltpu.VMEM(stack, BF16),
-            pltpu.VMEM((slices, pl.cdiv(nx, BLOCK), ny, 16 * views), F32),
-            pltpu.VMEM((slices, pl.cdiv(nx, BLOCK), 16 * views, ny), F32),
-            pltpu.SemaphoreType.DMA((slices,)),
+            pltpu.VMEM((slices * views, nx, ny), BF16),
+            pltpu.VMEM((slices, narrow, views * NARROW, ny), BF16),
+            pltpu.VMEM((max(ny // block - 1, 1), nx, 16 * slices * views), F32),
+            pltpu.SemaphoreType.DMA((slices - 1 + narrow,)),
         ],
         compiler_params=pltpu.CompilerParams(vmem_limit_bytes=VMEM_LIMIT),
         name="backproject",

time: 34.4 us -> 34.2 us (level)
  no operation moved by 1% of the time
where the time goes in v4:
time: 34.2 us; the launch traced here: 34.1 us
  blocking collectives  25.4 us (74%)
  Pallas kernels  8.67 us (25%)
    all_to_all x1, blocking collectives, local(): lax.all_to_all(wire.reshape(owners, held, lanes), 'slab', 0, 0, tiled=True)  15.3 us
    all_to_all x1, blocking collectives, local(): lax.all_to_all(back.reshape(owners, per_owner, lanes), 'slab', 0, 0, tile...  10 us
    pallas_call x1, Pallas kernels, local(): pl.pallas_call(functools.partial(backward_kernel, views, slices, bins, ow...  4.3 us
    pallas_call x1, Pallas kernels, local(): pl.pallas_call(functools.partial(forward_kernel, views, slices, bins), in...  3.37 us
    pallas_call x1, Pallas kernels, local(): pl.pallas_call(functools.partial(middle_kernel, views, slices, bins, owne...  1 us

profile of v4, /device:TPU:0, one launch (start us, length us, event | category | flops | bytes accessed | tf_op | source)
XLA Modules:
  0.0 34.1 jit_solution(12175376399884848004)
XLA Ops:
  0.0 0.0 copy-start.2
  0.0 0.0 copy-start.1
  0.0 0.0 copy-start.3
  0.0 0.0 copy-start
  0.0 3.4 %project.1 = (bf16[512,128]{1,0:T(8,128)(2,1)S(1)}, f32[4,512,512]{2,1,0:T(8,128)S(1)}, bf16[4,128,256]{2,1,0:T(8,128)(2,1)S(1)}, bf16[2,512,512]{2,1,0:T(8,128)...) custom-call(f32[4,512,512]{2,1,0:T(8,128)} %image_hbm.1, ...), custom_call_target="tpu_custom_call" | custom-call | tf_op jit(solution)/shard_map/project/pallas_call | solution.py:349
  3.4 15.3 %all_to_all.10 = bf16[32,16,128]{2,1,0:T(8,128)(2,1)S(1)} all-to-all(bf16[32,16,128]{2,1,0:T(8,128)(2,1)S(1)} %bitcast.11), channel_id=1, replica_groups=mesh['view'=1,'slab'=32] {'slab'}, dimensions={0} | all-to-all | bytes 262144 | tf_op jit(solution)/shard_map/all_to_all | solution.py:371
  18.7 0.0 copy-done.2
  18.7 0.0 copy-done.1
  18.7 0.0 copy-done.3
  18.8 1.0 %compare.1 = bf16[512,128]{1,0:T(8,128)(2,1)S(1)} custom-call(bf16[512,128]{1,0:T(8,128)(2,1)S(1)} %bitcast.7, f32[2,128,128]{2,1,0:T(8,128)S(1)} %copy-done.3, f32[512,128]{1,0:T(8,128)S(1)} %bitcast.9, s32[512,128]{1,0:T(8,128)S(1)} %bitcast.10), custom_call_target="tpu_custom_call" | custom-call | bytes 41943040 | tf_op jit(solution)/shard_map/compare/pallas_call | solution.py:376
  19.8 10.0 %all_to_all.11 = bf16[32,16,128]{2,1,0:T(8,128)(2,1)S(1)} all-to-all(bf16[32,16,128]{2,1,0:T(8,128)(2,1)S(1)} %bitcast.8), channel_id=1, replica_groups=mesh['view'=1,'slab'=32] {'slab'}, dimensions={0} | all-to-all | bytes 262144 | tf_op jit(solution)/shard_map/all_to_all | solution.py:394
  29.8 0.0 copy-done
  29.8 4.3 %backproject.1 = f32[4,512,512]{2,1,0:T(8,128)} custom-call(bf16[512,128]{1,0:T(8,128)(2,1)S(1)} %bitcast.6, bf16[2,16,512]{2,1,0:T(8,128)(2,1)S(1)} %get-tuple-element.14.refs_1_, bf16[2,512,128]{2,1,0:T(8,128)(2,1)S(1)} %get-tuple-element.15.refs_2_, bf16[2,512,512]{2,1,0:T(8,128)(2,1)S(1)} %get-tuple-element.16.refs_3_, ...), custom_call_target="tpu_custom_call" | custom-call | tf_op jit(solution)/shard_map/backproject/pallas_call | solution.py:402
Async XLA Ops:
  0.0 18.7 %copy-start.2 = (s32[2,16,16,128]{3,2,1,0:T(8,128)S(1)}, s32[2,16,16,128]{3,2,1,0:T(8,128)}, u32[]{:S(2)}) copy-start(s32[2,16,16,128]{3,2,1,0:T(8,128)} %param.15) | copy-start | bytes 786436
  0.0 18.7 %copy-start.1 = (f32[2,16,16,128]{3,2,1,0:T(8,128)S(1)}, f32[2,16,16,128]{3,2,1,0:T(8,128)}, u32[]{:S(2)}) copy-start(f32[2,16,16,128]{3,2,1,0:T(8,128)} %param.14) | copy-start | bytes 786436
  0.0 18.7 %copy-start.3 = (f32[2,128,128]{2,1,0:T(8,128)S(1)}, f32[2,128,128]{2,1,0:T(8,128)}, u32[]{:S(2)}) copy-start(f32[2,128,128]{2,1,0:T(8,128)} %mix.1) | copy-start | bytes 393220
  0.0 29.8 %copy-start = (f32[4,512,512]{2,1,0:T(8,128)S(1)}, f32[4,512,512]{2,1,0:T(8,128)}, u32[]{:S(2)}) copy-start(f32[4,512,512]{2,1,0:T(8,128)} %refs_8_.1) | copy-start | bytes 12582916

commit v5 on v4

--- a/solution.py
+++ b/solution.py
@@ -11,7 +11,7 @@
 VMEM_LIMIT = 24 * 1024 * 1024
 FIRST_LIMIT = 60 * 1024 * 1024
 BLOCK, NARROW, BAND, NEAR = 256, 128, 3, 16
-POWER, OFFSET = 20.75, 86.5
+POWER, OFFSET = 41.5, 86.3
 NN = (((1,), (0,)), ((), ()))
 NT = (((1,), (1,)), ((), ()))
 
@@ -32,37 +32,25 @@
 
 
 def encode(x):
-    return jnp.exp(POWER * jnp.log(1.0 + 2.0 * x) - OFFSET).astype(BF16)
+    place = POWER * jnp.log(1.0 + 2.0 * x) - 2.0 * OFFSET
+    size = jnp.exp(jnp.abs(place) - OFFSET)
+    return jnp.where(place < 0.0, -size, size).astype(BF16)
 
 
 def decode(y):
-    return 0.5 * jnp.exp((jnp.log(y.astype(F32)) + OFFSET) * (1.0 / POWER)) - 0.5
+    y = y.astype(F32)
+    size = jnp.log(jnp.abs(y)) + OFFSET
+    place = jnp.where(y < 0.0, -size, size)
+    return 0.5 * jnp.exp((place + 2.0 * OFFSET) * (1.0 / POWER)) - 0.5
 
 
 def in_hbm(x):
     return pltpu.with_memory_space_constraint(x, pltpu.HBM)
 
 
-def banded(rows, matrix, edge, between=1):
-    cells = matrix.shape[0]
-    block = min(BLOCK, cells)
-    parts = [
-        dot(rows[:, at : at + block], matrix[at : at + block, at : at + block])
-        for at in range(0, cells, block)
-    ]
-    for n in range(1, len(parts)):
-        at = n * block
-        extra = dot(rows[:, at - NEAR : at + NEAR], corner(edge[n * between - 1]).astype(BF16))
-        parts[n - 1] = jnp.concatenate(
-            [parts[n - 1][:, : block - 128], parts[n - 1][:, block - 128 :] + extra[:, :128]], axis=1
-        )
-        parts[n] = jnp.concatenate([parts[n][:, :128] + extra[:, 128:], parts[n][:, 128:]], axis=1)
-    return jnp.concatenate(parts, axis=1)
-
-
 def forward_kernel(
     views, slices, bins, image_hbm, rx_hbm, ry_hbm, tof_hbm,
-    out, image, strips_x, ryt, edge_y, edge_x, toft, tof, rx, ry, sems,
+    out, image, strips_x, ryt, edge_y, edge_x, toft, tof, rx, ry, along, rotated, sems,
 ):
     cells = rx.shape[1]
     block = min(BLOCK, cells)
@@ -78,9 +66,9 @@
         return copies
 
     images = [(image_hbm.at[z], image.at[z]) for z in range(slices)]
-    groups = [[(tof_hbm, tof)] + band(rx_hbm, rx, edge_x, NARROW)]
-    groups += [images[:1], images[1:2], band(ry_hbm, ry, edge_y, block)]
-    groups += [[pair] for pair in images[2:]]
+    groups = [band(ry_hbm, ry, edge_y, block), images[:1]]
+    groups += [[(tof_hbm, tof)] + band(rx_hbm, rx, edge_x, NARROW)]
+    groups += [[pair] for pair in images[1:]]
     loads, n = [], 0
     for group in groups:
         loads.append([pltpu.make_async_copy(*pair, sems.at[n + i]) for i, pair in enumerate(group)])
@@ -93,47 +81,97 @@
         for load in next(loads):
             load.wait()
 
-    rows = views * bins
     per_row = toft.shape[2] // bins
-    partial = []
-
-    def add_slice(z):
+    edges = range(block, cells, block)
+    integrals = []
+
+    def along_second(z):
+        low = image[z].astype(BF16)
+        extra = [dot(low[:, e - 128 : e + 128], corners[n]) for n, e in enumerate(edges)]
+        for v in range(views):
+            parts = [
+                dot(low[:, at : at + block], ry[v, at : at + block, at : at + block])
+                for at in range(0, cells, block)
+            ]
+            parts = add_sides(parts, extra, 16 * v)
+            for n, part in enumerate(parts):
+                along[z * views + v, :, n * block : (n + 1) * block] = part.astype(BF16)
+
+    def along_first(z):
+        for v in range(views):
+            i = z * views + v
+            parts = [
+                dot(rx[v, at : at + block, at : at + block], along[i, at : at + block, :])
+                for at in range(0, cells, block)
+            ]
+            for n, e in enumerate(edges):
+                above, below = sides[v][n]
+                near = along[i, e - 16 : e + 16, :].astype(F32)
+                last, first = parts[n][-8:], parts[n + 1][:8]
+                for m in range(BAND):
+                    last += above[m] * near[16 + m : 17 + m]
+                    first += below[m] * near[15 - m : 16 - m]
+                parts[n] = jnp.concatenate([parts[n][:-8], last], axis=0)
+                parts[n + 1] = jnp.concatenate([first, parts[n + 1][8:]], axis=0)
+            for n, part in enumerate(parts):
+                rotated[i, n * block : (n + 1) * block, :] = part.astype(BF16)
+
+    def along_rays(z):
+        for v in range(views):
+            integrals.append(dot(tof[v], rotated[z * views + v]))
+
+    arrive()
+    corners = []
+    for n in range(len(edges)):
+        near = [corner(edge_y[v, n])[:, 120:136] for v in range(views)]
+        near = jnp.concatenate(near + [jnp.zeros((2 * NEAR, 128 - 16 * views), F32)], axis=1)
+        above = jnp.zeros((128 - NEAR, 128), F32)
+        corners.append(jnp.concatenate([above, near, above], axis=0).astype(BF16))
+    arrive()
+    along_second(0)
+    arrive()
+    between = block // NARROW
+    sides = [
+        [corner_columns(edge_x[v, (n + 1) * between - 1], cells) for n in range(len(edges))]
+        for v in range(views)
+    ]
+    along_first(0)
+    for z in range(1, slices):
         arrive()
-        both = dot(weights, image[z].astype(BF16))
-        partial.append(both[:rows] + both[rows:])
-
-    arrive()
-    pairs = [halves(banded(tof[v], rx.at[v], edge_x.at[v], block // NARROW)) for v in range(views)]
-    weights = jnp.concatenate([p[0] for p in pairs] + [p[1] for p in pairs], axis=0)
-    add_slice(0)
-    for v in range(views):
-        for n, at in enumerate(range(0, cells, NARROW)):
-            strips_x[n, :, v * NARROW : (v + 1) * NARROW] = rx[v, at : at + NARROW, at : at + NARROW].T
-            if at % block > 0:
-                edge_x[v, n - 1] = rx[v, at - NEAR : at + NEAR, at - 128 : at + 128]
-    add_slice(1)
-    arrive()
-    for v in range(views):
-        toft[v] = jnp.concatenate([tof[v]] * per_row, axis=0).T
-        for at in range(0, cells, block):
-            here = slice(at, at + block)
-            ryt[v, here, here] = ry[v, here, here].T
-    for z in range(2, slices):
-        add_slice(z)
-    per_view = []
-    for v in range(views):
-        mine = jnp.concatenate([p[v * bins : (v + 1) * bins] for p in partial], axis=0)
-        both = banded(jnp.concatenate(halves(mine), axis=0), ry.at[v], edge_y.at[v])
-        per_view.append(both[: slices * bins] + both[slices * bins :])
-    joined = jnp.concatenate(
-        [
-            per_view[v][s * bins : (s + 1) * bins]
-            for s in range(slices)
-            for v in range(views)
-        ],
-        axis=0,
-    )
-    out[...] = encode(joined.T)
+        along_second(z)
+        along_rays(z - 1)
+        along_first(z)
+        if z == 1:
+            for v in range(views):
+                for n, at in enumerate(range(0, cells, NARROW)):
+                    strips_x[n, :, v * NARROW : (v + 1) * NARROW] = rx[
+                        v, at : at + NARROW, at : at + NARROW
+                    ].T
+                    if at % block > 0:
+                        edge_x[v, n - 1] = rx[v, at - NEAR : at + NEAR, at - 128 : at + 128]
+        if z == min(2, slices - 1):
+            for v in range(views):
+                toft[v] = jnp.concatenate([tof[v]] * per_row, axis=0).T
+                for at in range(0, cells, block):
+                    here = slice(at, at + block)
+                    ryt[v, here, here] = ry[v, here, here].T
+    along_rays(slices - 1)
+    out[...] = encode(jnp.concatenate(integrals, axis=0).T)
+
+
+def add_sides(parts, extra, spot):
+    parts = list(parts)
+    for n, columns in enumerate(extra):
+        lane = lax.broadcasted_iota(jnp.int32, columns.shape, 1)
+        columns = pltpu.roll(columns, (120 - spot) % 128, 1)
+        left, right = parts[n], parts[n + 1]
+        parts[n] = jnp.concatenate(
+            [left[:, :-128], left[:, -128:] + jnp.where(lane >= 120, columns, 0.0)], axis=1
+        )
+        parts[n + 1] = jnp.concatenate(
+            [right[:, :128] + jnp.where(lane < 8, columns, 0.0), right[:, 128:]], axis=1
+        )
+    return parts
 
 
 def swap_blocks(parts, width):
@@ -276,17 +314,7 @@
                 dot(frames[i, :, at : at + block], ryt[v, at : at + block, at : at + block])
                 for at in range(0, cells, block)
             ]
-            for n in range(len(edges)):
-                extra = turned[n]
-                lane = lax.broadcasted_iota(jnp.int32, extra.shape, 1)
-                extra = pltpu.roll(extra, (120 - 16 * (v * slices + z)) % 128, 1)
-                left, right = parts[n], parts[n + 1]
-                parts[n] = jnp.concatenate(
-                    [left[:, :-128], left[:, -128:] + jnp.where(lane >= 120, extra, 0.0)], axis=1
-                )
-                parts[n + 1] = jnp.concatenate(
-                    [right[:, :128] + jnp.where(lane < 8, extra, 0.0), right[:, 128:]], axis=1
-                )
+            parts = add_sides(parts, [turned[n] for n in range(len(edges))], 16 * (v * slices + z))
             for n, part in enumerate(parts):
                 part = part.astype(BF16)
                 for w in range(cells // NARROW):
@@ -363,6 +391,8 @@
         scratch_shapes=[
             pltpu.VMEM(resample_x.shape, BF16),
             pltpu.VMEM(resample_y.shape, BF16),
+            pltpu.VMEM((slices * views, nx, ny), BF16),
+            pltpu.VMEM((slices * views, nx, ny), BF16),
             pltpu.SemaphoreType.DMA((4 * (nx // block) - 1 + slices,)),
         ],
         compiler_params=pltpu.CompilerParams(vmem_limit_bytes=VMEM_LIMIT),

time: 34.2 us -> 36.6 us (1.070)
  Pallas kernels: 8.67 us -> 11.1 us
    pallas_call x1, Pallas kernels: 3.37 us -> 5.73 us  [local(): pl.pallas_call(functools.partial(forward_kernel, views, slices, bins), in...]
where the time goes in v5:
time: 36.6 us; the launch traced here: 36.5 us
  blocking collectives  25.4 us (69%)
  Pallas kernels  11.1 us (30%)
    all_to_all x1, blocking collectives, local(): lax.all_to_all(wire.reshape(owners, held, lanes), 'slab', 0, 0, tiled=True)  15.3 us
    all_to_all x1, blocking collectives, local(): lax.all_to_all(back.reshape(owners, per_owner, lanes), 'slab', 0, 0, tile...  10 us
    pallas_call x1, Pallas kernels, local(): pl.pallas_call(functools.partial(forward_kernel, views, slices, bins), in...  5.73 us
    pallas_call x1, Pallas kernels, local(): pl.pallas_call(functools.partial(backward_kernel, views, slices, bins, ow...  4.29 us
    pallas_call x1, Pallas kernels, local(): pl.pallas_call(functools.partial(middle_kernel, views, slices, bins, owne...  1.05 us

profile of v5, /device:TPU:0, one launch (start us, length us, event | category | flops | bytes accessed | tf_op | source)
XLA Modules:
  0.0 36.5 jit_solution(12286614523533255477)
XLA Ops:
  0.0 0.0 copy-start.2
  0.0 0.0 copy-start.1
  0.0 0.0 copy-start.3
  0.0 0.0 copy-start
  0.0 5.7 %project.1 = (bf16[512,128]{1,0:T(8,128)(2,1)S(1)}, f32[4,512,512]{2,1,0:T(8,128)S(1)}, bf16[4,128,256]{2,1,0:T(8,128)(2,1)S(1)}, bf16[2,512,512]{2,1,0:T(8,128)...) custom-call(f32[4,512,512]{2,1,0:T(8,128)} %image_hbm.1, ...), custom_call_target="tpu_custom_call" | custom-call | tf_op jit(solution)/shard_map/project/pallas_call | solution.py:377
  5.7 15.3 %all_to_all.10 = bf16[32,16,128]{2,1,0:T(8,128)(2,1)S(1)} all-to-all(bf16[32,16,128]{2,1,0:T(8,128)(2,1)S(1)} %bitcast.11), channel_id=1, replica_groups=mesh['view'=1,'slab'=32] {'slab'}, dimensions={0} | all-to-all | bytes 262144 | tf_op jit(solution)/shard_map/all_to_all | solution.py:401
  21.1 0.0 copy-done.2
  21.1 0.0 copy-done.1
  21.1 0.0 copy-done.3
  21.1 1.0 %compare.1 = bf16[512,128]{1,0:T(8,128)(2,1)S(1)} custom-call(bf16[512,128]{1,0:T(8,128)(2,1)S(1)} %bitcast.7, f32[2,128,128]{2,1,0:T(8,128)S(1)} %copy-done.3, f32[512,128]{1,0:T(8,128)S(1)} %bitcast.9, s32[512,128]{1,0:T(8,128)S(1)} %bitcast.10), custom_call_target="tpu_custom_call" | custom-call | bytes 41943040 | tf_op jit(solution)/shard_map/compare/pallas_call | solution.py:406
  22.2 10.0 %all_to_all.11 = bf16[32,16,128]{2,1,0:T(8,128)(2,1)S(1)} all-to-all(bf16[32,16,128]{2,1,0:T(8,128)(2,1)S(1)} %bitcast.8), channel_id=1, replica_groups=mesh['view'=1,'slab'=32] {'slab'}, dimensions={0} | all-to-all | bytes 262144 | tf_op jit(solution)/shard_map/all_to_all | solution.py:424
  32.2 0.0 copy-done
  32.2 4.3 %backproject.1 = f32[4,512,512]{2,1,0:T(8,128)} custom-call(bf16[512,128]{1,0:T(8,128)(2,1)S(1)} %bitcast.6, bf16[2,16,512]{2,1,0:T(8,128)(2,1)S(1)} %get-tuple-element.14.refs_1_, bf16[2,512,128]{2,1,0:T(8,128)(2,1)S(1)} %get-tuple-element.15.refs_2_, bf16[2,512,512]{2,1,0:T(8,128)(2,1)S(1)} %get-tuple-element.16.refs_3_, ...), custom_call_target="tpu_custom_call" | custom-call | tf_op jit(solution)/shard_map/backproject/pallas_call | solution.py:432
Async XLA Ops:
  0.0 21.1 %copy-start.2 = (s32[2,16,16,128]{3,2,1,0:T(8,128)S(1)}, s32[2,16,16,128]{3,2,1,0:T(8,128)}, u32[]{:S(2)}) copy-start(s32[2,16,16,128]{3,2,1,0:T(8,128)} %param.15) | copy-start | bytes 786436
  0.0 21.1 %copy-start.1 = (f32[2,16,16,128]{3,2,1,0:T(8,128)S(1)}, f32[2,16,16,128]{3,2,1,0:T(8,128)}, u32[]{:S(2)}) copy-start(f32[2,16,16,128]{3,2,1,0:T(8,128)} %param.14) | copy-start | bytes 786436
  0.0 21.1 %copy-start.3 = (f32[2,128,128]{2,1,0:T(8,128)S(1)}, f32[2,128,128]{2,1,0:T(8,128)}, u32[]{:S(2)}) copy-start(f32[2,128,128]{2,1,0:T(8,128)} %mix.1) | copy-start | bytes 393220
  0.0 32.2 %copy-start = (f32[4,512,512]{2,1,0:T(8,128)S(1)}, f32[4,512,512]{2,1,0:T(8,128)}, u32[]{:S(2)}) copy-start(f32[4,512,512]{2,1,0:T(8,128)} %refs_8_.1) | copy-start | bytes 12582916

commit v6 on v5

--- a/solution.py
+++ b/solution.py
@@ -34,7 +34,7 @@
 def encode(x):
     place = POWER * jnp.log(1.0 + 2.0 * x) - 2.0 * OFFSET
     size = jnp.exp(jnp.abs(place) - OFFSET)
-    return jnp.where(place < 0.0, -size, size).astype(BF16)
+    return jnp.where(place < 0.0, -size, size)
 
 
 def decode(y):
@@ -66,7 +66,9 @@
         return copies
 
     images = [(image_hbm.at[z], image.at[z]) for z in range(slices)]
-    groups = [band(ry_hbm, ry, edge_y, block), images[:1]]
+    top, bottom = pl.ds(0, block), pl.ds(block, cells - block)
+    groups = [band(ry_hbm, ry, edge_y, block) + [(image_hbm.at[0, top], image.at[0, top])]]
+    groups += [[(image_hbm.at[0, bottom], image.at[0, bottom])]]
     groups += [[(tof_hbm, tof)] + band(rx_hbm, rx, edge_x, NARROW)]
     groups += [[pair] for pair in images[1:]]
     loads, n = [], 0
@@ -83,10 +85,10 @@
 
     per_row = toft.shape[2] // bins
     edges = range(block, cells, block)
-    integrals = []
-
-    def along_second(z):
-        low = image[z].astype(BF16)
+    coded = []
+
+    def along_second(z, rows=slice(None)):
+        low = image[z, rows].astype(BF16)
         extra = [dot(low[:, e - 128 : e + 128], corners[n]) for n, e in enumerate(edges)]
         for v in range(views):
             parts = [
@@ -95,7 +97,7 @@
             ]
             parts = add_sides(parts, extra, 16 * v)
             for n, part in enumerate(parts):
-                along[z * views + v, :, n * block : (n + 1) * block] = part.astype(BF16)
+                along[z * views + v, rows, n * block : (n + 1) * block] = part.astype(BF16)
 
     def along_first(z):
         for v in range(views):
@@ -118,7 +120,7 @@
 
     def along_rays(z):
         for v in range(views):
-            integrals.append(dot(tof[v], rotated[z * views + v]))
+            coded.append(encode(dot(tof[v], rotated[z * views + v])))
 
     arrive()
     corners = []
@@ -127,20 +129,21 @@
         near = jnp.concatenate(near + [jnp.zeros((2 * NEAR, 128 - 16 * views), F32)], axis=1)
         above = jnp.zeros((128 - NEAR, 128), F32)
         corners.append(jnp.concatenate([above, near, above], axis=0).astype(BF16))
+    along_second(0, slice(0, block))
     arrive()
-    along_second(0)
+    along_second(0, slice(block, cells))
     arrive()
     between = block // NARROW
     sides = [
         [corner_columns(edge_x[v, (n + 1) * between - 1], cells) for n in range(len(edges))]
         for v in range(views)
     ]
-    along_first(0)
     for z in range(1, slices):
         arrive()
         along_second(z)
-        along_rays(z - 1)
-        along_first(z)
+        along_first(z - 1)
+        if z > 1:
+            along_rays(z - 2)
         if z == 1:
             for v in range(views):
                 for n, at in enumerate(range(0, cells, NARROW)):
@@ -155,8 +158,10 @@
                 for at in range(0, cells, block):
                     here = slice(at, at + block)
                     ryt[v, here, here] = ry[v, here, here].T
+    along_rays(slices - 2)
+    along_first(slices - 1)
     along_rays(slices - 1)
-    out[...] = encode(jnp.concatenate(integrals, axis=0).T)
+    out[...] = jnp.concatenate(coded, axis=0).T.astype(BF16)
 
 
 def add_sides(parts, extra, spot):
@@ -393,7 +398,7 @@
             pltpu.VMEM(resample_y.shape, BF16),
             pltpu.VMEM((slices * views, nx, ny), BF16),
             pltpu.VMEM((slices * views, nx, ny), BF16),
-            pltpu.SemaphoreType.DMA((4 * (nx // block) - 1 + slices,)),
+            pltpu.SemaphoreType.DMA((4 * (nx // block) + slices,)),
         ],
         compiler_params=pltpu.CompilerParams(vmem_limit_bytes=VMEM_LIMIT),
         name="project",

time: 36.6 us -> 36.5 us (level)
  no operation moved by 1% of the time
where the time goes in v6:
time: 36.5 us; the launch traced here: 36.3 us
  blocking collectives  25.3 us (69%)
  Pallas kernels  10.9 us (30%)
    all_to_all x1, blocking collectives, local(): lax.all_to_all(wire.reshape(owners, held, lanes), 'slab', 0, 0, tiled=True)  15.3 us
    all_to_all x1, blocking collectives, local(): lax.all_to_all(back.reshape(owners, per_owner, lanes), 'slab', 0, 0, tile...  10 us
    pallas_call x1, Pallas kernels, local(): pl.pallas_call(functools.partial(forward_kernel, views, slices, bins), in...  5.56 us
    pallas_call x1, Pallas kernels, local(): pl.pallas_call(functools.partial(backward_kernel, views, slices, bins, ow...  4.3 us
    pallas_call x1, Pallas kernels, local(): pl.pallas_call(functools.partial(middle_kernel, views, slices, bins, owne...  1.05 us

profile of v6, /device:TPU:0, one launch (start us, length us, event | category | flops | bytes accessed | tf_op | source)
XLA Modules:
  0.0 36.3 jit_solution(94905976797702260)
XLA Ops:
  0.0 0.0 copy-start.2
  0.0 0.0 copy-start.1
  0.0 0.0 copy-start.3
  0.0 0.0 copy-start
  0.0 5.6 %project.1 = (bf16[512,128]{1,0:T(8,128)(2,1)S(1)}, f32[4,512,512]{2,1,0:T(8,128)S(1)}, bf16[4,128,256]{2,1,0:T(8,128)(2,1)S(1)}, bf16[2,512,512]{2,1,0:T(8,128)...) custom-call(f32[4,512,512]{2,1,0:T(8,128)} %image_hbm.1, ...), custom_call_target="tpu_custom_call" | custom-call | tf_op jit(solution)/shard_map/project/pallas_call | solution.py:382
  5.6 15.3 %all_to_all.10 = bf16[32,16,128]{2,1,0:T(8,128)(2,1)S(1)} all-to-all(bf16[32,16,128]{2,1,0:T(8,128)(2,1)S(1)} %bitcast.11), channel_id=1, replica_groups=mesh['view'=1,'slab'=32] {'slab'}, dimensions={0} | all-to-all | bytes 262144 | tf_op jit(solution)/shard_map/all_to_all | solution.py:406
  20.9 0.0 copy-done.2
  20.9 0.0 copy-done.1
  20.9 0.0 copy-done.3
  20.9 1.0 %compare.1 = bf16[512,128]{1,0:T(8,128)(2,1)S(1)} custom-call(bf16[512,128]{1,0:T(8,128)(2,1)S(1)} %bitcast.7, f32[2,128,128]{2,1,0:T(8,128)S(1)} %copy-done.3, f32[512,128]{1,0:T(8,128)S(1)} %bitcast.9, s32[512,128]{1,0:T(8,128)S(1)} %bitcast.10), custom_call_target="tpu_custom_call" | custom-call | bytes 41943040 | tf_op jit(solution)/shard_map/compare/pallas_call | solution.py:411
  22.0 10.0 %all_to_all.11 = bf16[32,16,128]{2,1,0:T(8,128)(2,1)S(1)} all-to-all(bf16[32,16,128]{2,1,0:T(8,128)(2,1)S(1)} %bitcast.8), channel_id=1, replica_groups=mesh['view'=1,'slab'=32] {'slab'}, dimensions={0} | all-to-all | bytes 262144 | tf_op jit(solution)/shard_map/all_to_all | solution.py:429
  32.0 0.0 copy-done
  32.0 4.3 %backproject.1 = f32[4,512,512]{2,1,0:T(8,128)} custom-call(bf16[512,128]{1,0:T(8,128)(2,1)S(1)} %bitcast.6, bf16[2,16,512]{2,1,0:T(8,128)(2,1)S(1)} %get-tuple-element.14.refs_1_, bf16[2,512,128]{2,1,0:T(8,128)(2,1)S(1)} %get-tuple-element.15.refs_2_, bf16[2,512,512]{2,1,0:T(8,128)(2,1)S(1)} %get-tuple-element.16.refs_3_, ...), custom_call_target="tpu_custom_call" | custom-call | tf_op jit(solution)/shard_map/backproject/pallas_call | solution.py:437
Async XLA Ops:
  0.0 20.9 %copy-start.2 = (s32[2,16,16,128]{3,2,1,0:T(8,128)S(1)}, s32[2,16,16,128]{3,2,1,0:T(8,128)}, u32[]{:S(2)}) copy-start(s32[2,16,16,128]{3,2,1,0:T(8,128)} %param.15) | copy-start | bytes 786436
  0.0 20.9 %copy-start.1 = (f32[2,16,16,128]{3,2,1,0:T(8,128)S(1)}, f32[2,16,16,128]{3,2,1,0:T(8,128)}, u32[]{:S(2)}) copy-start(f32[2,16,16,128]{3,2,1,0:T(8,128)} %param.14) | copy-start | bytes 786436
  0.0 20.9 %copy-start.3 = (f32[2,128,128]{2,1,0:T(8,128)S(1)}, f32[2,128,128]{2,1,0:T(8,128)}, u32[]{:S(2)}) copy-start(f32[2,128,128]{2,1,0:T(8,128)} %mix.1) | copy-start | bytes 393220
  0.0 32.0 %copy-start = (f32[4,512,512]{2,1,0:T(8,128)S(1)}, f32[4,512,512]{2,1,0:T(8,128)}, u32[]{:S(2)}) copy-start(f32[4,512,512]{2,1,0:T(8,128)} %refs_8_.1) | copy-start | bytes 12582916

commit v7 on v6

--- a/solution.py
+++ b/solution.py
@@ -69,8 +69,8 @@
     top, bottom = pl.ds(0, block), pl.ds(block, cells - block)
     groups = [band(ry_hbm, ry, edge_y, block) + [(image_hbm.at[0, top], image.at[0, top])]]
     groups += [[(image_hbm.at[0, bottom], image.at[0, bottom])]]
-    groups += [[(tof_hbm, tof)] + band(rx_hbm, rx, edge_x, NARROW)]
-    groups += [[pair] for pair in images[1:]]
+    groups += [images[1:2], [(tof_hbm, tof)] + band(rx_hbm, rx, edge_x, NARROW)]
+    groups += [[pair] for pair in images[2:]]
     loads, n = [], 0
     for group in groups:
         loads.append([pltpu.make_async_copy(*pair, sems.at[n + i]) for i, pair in enumerate(group)])
@@ -132,15 +132,16 @@
     along_second(0, slice(0, block))
     arrive()
     along_second(0, slice(block, cells))
-    arrive()
     between = block // NARROW
-    sides = [
-        [corner_columns(edge_x[v, (n + 1) * between - 1], cells) for n in range(len(edges))]
-        for v in range(views)
-    ]
     for z in range(1, slices):
         arrive()
         along_second(z)
+        if z == 1:
+            arrive()
+            sides = [
+                [corner_columns(edge_x[v, (n + 1) * between - 1], cells) for n in range(len(edges))]
+                for v in range(views)
+            ]
         along_first(z - 1)
         if z > 1:
             along_rays(z - 2)

time: 36.5 us -> 36.7 us (level)
  no operation moved by 1% of the time
where the time goes in v7:
time: 36.7 us; the launch traced here: 36.5 us
  blocking collectives  25.4 us (69%)
  Pallas kernels  11.1 us (30%)
    all_to_all x1, blocking collectives, local(): lax.all_to_all(wire.reshape(owners, held, lanes), 'slab', 0, 0, tiled=True)  15.4 us
    all_to_all x1, blocking collectives, local(): lax.all_to_all(back.reshape(owners, per_owner, lanes), 'slab', 0, 0, tile...  10 us
    pallas_call x1, Pallas kernels, local(): pl.pallas_call(functools.partial(forward_kernel, views, slices, bins), in...  5.75 us
    pallas_call x1, Pallas kernels, local(): pl.pallas_call(functools.partial(backward_kernel, views, slices, bins, ow...  4.3 us
    pallas_call x1, Pallas kernels, local(): pl.pallas_call(functools.partial(middle_kernel, views, slices, bins, owne...  1.05 us

profile of v7, /device:TPU:0, one launch (start us, length us, event | category | flops | bytes accessed | tf_op | source)
XLA Modules:
  0.0 36.5 jit_solution(17969574438768655781)
XLA Ops:
  0.0 0.0 copy-start.2
  0.0 0.0 copy-start.1
  0.0 0.0 copy-start.3
  0.0 0.0 copy-start
  0.0 5.7 %project.1 = (bf16[512,128]{1,0:T(8,128)(2,1)S(1)}, f32[4,512,512]{2,1,0:T(8,128)S(1)}, bf16[4,128,256]{2,1,0:T(8,128)(2,1)S(1)}, bf16[2,512,512]{2,1,0:T(8,128)...) custom-call(f32[4,512,512]{2,1,0:T(8,128)} %image_hbm.1, ...), custom_call_target="tpu_custom_call" | custom-call | tf_op jit(solution)/shard_map/project/pallas_call | solution.py:383
  5.8 15.4 %all_to_all.10 = bf16[32,16,128]{2,1,0:T(8,128)(2,1)S(1)} all-to-all(bf16[32,16,128]{2,1,0:T(8,128)(2,1)S(1)} %bitcast.11), channel_id=1, replica_groups=mesh['view'=1,'slab'=32] {'slab'}, dimensions={0} | all-to-all | bytes 262144 | tf_op jit(solution)/shard_map/all_to_all | solution.py:407
  21.1 0.0 copy-done.2
  21.1 0.0 copy-done.1
  21.1 0.0 copy-done.3
  21.1 1.0 %compare.1 = bf16[512,128]{1,0:T(8,128)(2,1)S(1)} custom-call(bf16[512,128]{1,0:T(8,128)(2,1)S(1)} %bitcast.7, f32[2,128,128]{2,1,0:T(8,128)S(1)} %copy-done.3, f32[512,128]{1,0:T(8,128)S(1)} %bitcast.9, s32[512,128]{1,0:T(8,128)S(1)} %bitcast.10), custom_call_target="tpu_custom_call" | custom-call | bytes 41943040 | tf_op jit(solution)/shard_map/compare/pallas_call | solution.py:412
  22.2 10.0 %all_to_all.11 = bf16[32,16,128]{2,1,0:T(8,128)(2,1)S(1)} all-to-all(bf16[32,16,128]{2,1,0:T(8,128)(2,1)S(1)} %bitcast.8), channel_id=1, replica_groups=mesh['view'=1,'slab'=32] {'slab'}, dimensions={0} | all-to-all | bytes 262144 | tf_op jit(solution)/shard_map/all_to_all | solution.py:430
  32.2 0.0 copy-done
  32.2 4.3 %backproject.1 = f32[4,512,512]{2,1,0:T(8,128)} custom-call(bf16[512,128]{1,0:T(8,128)(2,1)S(1)} %bitcast.6, bf16[2,16,512]{2,1,0:T(8,128)(2,1)S(1)} %get-tuple-element.14.refs_1_, bf16[2,512,128]{2,1,0:T(8,128)(2,1)S(1)} %get-tuple-element.15.refs_2_, bf16[2,512,512]{2,1,0:T(8,128)(2,1)S(1)} %get-tuple-element.16.refs_3_, ...), custom_call_target="tpu_custom_call" | custom-call | tf_op jit(solution)/shard_map/backproject/pallas_call | solution.py:438
Async XLA Ops:
  0.0 21.1 %copy-start.2 = (s32[2,16,16,128]{3,2,1,0:T(8,128)S(1)}, s32[2,16,16,128]{3,2,1,0:T(8,128)}, u32[]{:S(2)}) copy-start(s32[2,16,16,128]{3,2,1,0:T(8,128)} %param.15) | copy-start | bytes 786436
  0.0 21.1 %copy-start.1 = (f32[2,16,16,128]{3,2,1,0:T(8,128)S(1)}, f32[2,16,16,128]{3,2,1,0:T(8,128)}, u32[]{:S(2)}) copy-start(f32[2,16,16,128]{3,2,1,0:T(8,128)} %param.14) | copy-start | bytes 786436
  0.0 21.1 %copy-start.3 = (f32[2,128,128]{2,1,0:T(8,128)S(1)}, f32[2,128,128]{2,1,0:T(8,128)}, u32[]{:S(2)}) copy-start(f32[2,128,128]{2,1,0:T(8,128)} %mix.1) | copy-start | bytes 393220
  0.0 32.2 %copy-start = (f32[4,512,512]{2,1,0:T(8,128)S(1)}, f32[4,512,512]{2,1,0:T(8,128)}, u32[]{:S(2)}) copy-start(f32[4,512,512]{2,1,0:T(8,128)} %refs_8_.1) | copy-start | bytes 12582916
